TPU v7x, 32 devices: a whole 2x2x4 slice. The times are simulated.
32 devices in a mesh: group: 2 (over x), ctx: 4 (over y, core), exp: 4 (over z).
Axes of the slice: x: 2, y: 2, z: 4, core: 2. Of those that a mesh axis runs over, the one named last changes fastest.
Arguments:
- queries: bfloat16 [1024, 1536], P(('group', 'ctx'), 'exp'), may hold values from -10.5 to 10.5
- keys: bfloat16 [1024, 512], P(('group', 'ctx'), 'exp'), may hold values from -4 to 4
- values: bfloat16 [1024, 512], P(('group', 'ctx'), 'exp'), may hold values from -6 to 6
- residual_in: bfloat16 [1024, 1536], P(('group', 'ctx', 'exp')), may hold values from -6 to 6
- doc_lengths: int32 [4], replicated, may hold values from 1 to 384, 1024 in all
- w_out: bfloat16 [1536, 1536], P('exp', 'group'), may hold values from -0.15625 to 0.15625
- norm_gain: float32 [1536], replicated, may hold values from 0.5 to 1.5
- router: bfloat16 [1536, 16], replicated, may hold values from -0.15625 to 0.15625
- expert_ids: int32 [1024, 6], P(('group', 'ctx', 'exp')), may hold values from 0 to 15, all different within a row; in each aligned block of 32 rows (0 to 31, 32 to 63, ...) at most 18 rows name the same one
- expert_gate_up: bfloat16 [16, 1536, 1024], P(('ctx', 'exp'), 'group'), may hold values from -0.15625 to 0.15625
- expert_down: bfloat16 [16, 1536, 512], P(('ctx', 'exp'), 'group'), may hold values from -0.25 to 0.25
- shared_gate_up: bfloat16 [1536, 2, 1024], P(None, None, 'exp'), may hold values from -0.15625 to 0.15625
- shared_down: bfloat16 [1024, 1536], P('exp'), may hold values from -0.1875 to 0.1875
Outputs:
- hidden_out: bfloat16 [1024, 1536], P(('group', 'ctx', 'exp'))
Inputs may be any that keep to these rules, and one draw needn't show every extreme that they name: `doc_lengths`: documents are packed back to back in stream order and one of them has length 384. `expert_ids`: within the 32 rows of one device along group+ctx+exp, no expert is named by more than 18 routes, a bound that some block reaches.
All inputs are finite; a program needn't handle non-finite values.
Results may differ from a plain program's by a relative error of at most 0.015.
Values may be sent and summed in bfloat16 or wider, within the bound.
A program may use at most 64 MiB of HBM per device.

v0:
```python
import math

import jax
import jax.numpy as jnp
from jax import lax
from jax.sharding import PartitionSpec as P

HEAD = 128


neg_big = -1e30


def passed_along(shard, axis, by):
    length = lax.axis_size(axis)
    pairs = [(i, i + by) for i in range(length) if 0 <= i + by < length]
    return lax.ppermute(shard, axis, pairs)


def doc_starts(positions, doc_lengths):
    doc_ends = jnp.cumsum(doc_lengths, dtype=jnp.int32)
    passed = (doc_ends[None, :] <= positions[:, None]).astype(jnp.int32)
    return jnp.sum(passed * doc_lengths[None, :], axis=1, dtype=jnp.int32)


def attend_block(soft_state, kv_block, source, query_heads, query_pos, query_start):
    run_max, run_sum, run_acc = soft_state
    rows_dev = kv_block.shape[1]
    key_pos = source * rows_dev + jnp.arange(rows_dev, dtype=jnp.int32)
    allowed = (key_pos[None, :] <= query_pos[:, None]) & (key_pos[None, :] >= query_start[:, None])
    key_heads = kv_block[0].reshape(rows_dev, -1, HEAD)
    value_heads = kv_block[1].reshape(rows_dev, -1, HEAD)
    scores = jnp.einsum(
        "tgpd,sgd->gpts", query_heads, key_heads, preferred_element_type=jnp.float32
    ) * (1.0 / math.sqrt(HEAD))
    scores = jnp.where(allowed, scores, neg_big)
    new_max = jnp.maximum(run_max, jnp.max(scores, axis=-1))
    weights = jnp.where(allowed, jnp.exp(scores - new_max[..., None]), 0.0)
    factor = jnp.exp(run_max - new_max)
    run_sum = run_sum * factor + jnp.sum(weights, axis=-1)
    run_acc = run_acc * factor[..., None] + jnp.einsum(
        "gpts,sgd->gptd",
        weights.astype(jnp.bfloat16),
        value_heads,
        preferred_element_type=jnp.float32,
    )
    return (new_max, run_sum, run_acc)


def visit_block(soft_state, kv_block, source, query_heads, query_pos, query_start):
    rows_dev = kv_block.shape[1]
    useful = (source >= 0) & (source * rows_dev + rows_dev - 1 >= query_start[0])

    def run_block(inner_state):
        return attend_block(inner_state, kv_block, source, query_heads, query_pos, query_start)

    def keep_block(inner_state):
        return inner_state

    return lax.cond(useful, run_block, keep_block, soft_state)


def on_device(
    queries,
    keys,
    values,
    residual_in,
    doc_lengths,
    w_out,
    norm_gain,
    router,
    expert_ids,
    expert_gate_up,
    expert_down,
    shared_gate_up,
    shared_down,
):
    rows_dev = queries.shape[0]
    kv_count = keys.shape[1] // HEAD
    per_kv = queries.shape[1] // HEAD // kv_count
    block_count = lax.axis_size("group") * lax.axis_size("ctx")
    look_back = min(32, block_count // 2)
    my_block = lax.axis_index("group") * lax.axis_size("ctx") + lax.axis_index("ctx")
    query_pos = my_block * rows_dev + jnp.arange(rows_dev, dtype=jnp.int32)
    query_start = doc_starts(query_pos, doc_lengths)
    query_heads = queries.reshape(rows_dev, kv_count, per_kv, HEAD)
    init_state = (
        jnp.full((kv_count, per_kv, rows_dev), neg_big, jnp.float32),
        jnp.zeros((kv_count, per_kv, rows_dev), jnp.float32),
        jnp.zeros((kv_count, per_kv, rows_dev, HEAD), jnp.float32),
    )
    kv_own = jnp.stack([keys, values])
    soft_state = visit_block(init_state, kv_own, my_block, query_heads, query_pos, query_start)

    def cycle_turn(turn_idx, loop_state):
        moving, inner_state = loop_state
        moving = passed_along(moving, ("group", "ctx"), 1)
        return (
            moving,
            visit_block(
                inner_state, moving, my_block - turn_idx, query_heads, query_pos, query_start
            ),
        )

    moving, soft_state = lax.fori_loop(1, look_back, cycle_turn, (kv_own, soft_state))
    run_max, run_sum, run_acc = soft_state
    attended = run_acc / run_sum[..., None]
    attended = jnp.transpose(attended, (2, 0, 1, 3)).reshape(rows_dev, -1).astype(jnp.bfloat16)
    out_full = lax.all_gather(w_out, "group", axis=1, tiled=True)
    tok_e = rows_dev // lax.axis_size("exp")
    picked = attended
    projected = lax.psum_scatter(
        jnp.dot(picked, out_full, preferred_element_type=jnp.float32).astype(jnp.bfloat16),
        "exp",
        scatter_dimension=0,
        tiled=True,
    ).astype(jnp.float32)
    stream = (residual_in.astype(jnp.float32) + projected).astype(jnp.bfloat16)
    stream_f = stream.astype(jnp.float32)
    normed = (
        stream_f
        * lax.rsqrt(jnp.mean(stream_f * stream_f, axis=-1, keepdims=True) + 1e-05)
        * norm_gain
    ).astype(jnp.bfloat16)
    expert_count = router.shape[1]
    route_count = expert_ids.shape[1]
    logits = jnp.dot(normed, router, preferred_element_type=jnp.float32)
    chosen = expert_ids[:, :, None] == jnp.arange(expert_count, dtype=jnp.int32)[None, None, :]
    picked_logits = jnp.sum(jnp.where(chosen, logits[:, None, :], 0.0), axis=-1)
    raw_gates = jax.nn.sigmoid(picked_logits)
    gate_probs = raw_gates / jnp.sum(raw_gates, axis=-1, keepdims=True)
    all_normed = lax.all_gather(normed, "exp", axis=0, tiled=True)
    shared_pre = jnp.einsum(
        "td,dkf->tkf", all_normed, shared_gate_up, preferred_element_type=jnp.float32
    )
    shared_act = (jax.nn.silu(shared_pre[:, 0]) * shared_pre[:, 1]).astype(jnp.bfloat16)
    picked = shared_act
    shared_out = lax.psum_scatter(
        jnp.dot(picked, shared_down, preferred_element_type=jnp.float32).astype(jnp.bfloat16),
        "exp",
        scatter_dimension=0,
        tiled=True,
    ).astype(jnp.float32)
    slot_count = max(2, 3 * tok_e * route_count // (2 * expert_count))
    flat_ids = expert_ids.reshape(-1)
    one_hot = (flat_ids[:, None] == jnp.arange(expert_count, dtype=jnp.int32)[None, :]).astype(
        jnp.int32
    )
    slot_of = jnp.sum(
        (jnp.cumsum(one_hot, axis=0, dtype=jnp.int32) - 1) * one_hot, axis=1, dtype=jnp.int32
    )
    target = flat_ids * slot_count + slot_of
    placing = (
        jnp.arange(expert_count * slot_count, dtype=jnp.int32)[:, None] == target[None, :]
    ).astype(jnp.bfloat16)
    placing = jnp.sum(placing.reshape(expert_count * slot_count, tok_e, route_count), axis=2)
    model_width = normed.shape[1]
    outgoing = (
        jnp.dot(placing, normed, preferred_element_type=jnp.float32)
        .astype(jnp.bfloat16)
        .reshape(expert_count, slot_count, model_width)
    )
    gate_up_full, down_full = (
        lax.all_gather(expert_gate_up, "group", axis=1, tiled=True),
        lax.all_gather(expert_down, "group", axis=1, tiled=True),
    )
    hidden_count = down_full.shape[2]
    local_experts = gate_up_full.shape[0]
    arrived = lax.all_to_all(outgoing, ("ctx", "exp"), split_axis=0, concat_axis=0, tiled=True)
    sources = arrived.shape[0] // local_experts
    grouped = arrived.reshape(sources, local_experts, arrived.shape[1], arrived.shape[2])
    pre_act = jnp.einsum(
        "nekd,edf->nekf", grouped, gate_up_full, preferred_element_type=jnp.float32
    )
    activated = (jax.nn.silu(pre_act[..., :hidden_count]) * pre_act[..., hidden_count:]).astype(
        jnp.bfloat16
    )
    result = jnp.einsum(
        "nekf,edf->nekd", activated, down_full, preferred_element_type=jnp.float32
    ).astype(jnp.bfloat16)
    returned = lax.all_to_all(
        result.reshape(arrived.shape), ("ctx", "exp"), split_axis=0, concat_axis=0, tiled=True
    )
    flat_back = returned.reshape(expert_count * slot_count, model_width)
    fetched = (
        jnp.take(flat_back, target, axis=0)
        .reshape(tok_e, route_count, model_width)
        .astype(jnp.float32)
    )
    routed = jnp.sum(gate_probs[:, :, None] * fetched, axis=1)
    return (stream_f + shared_out + routed).astype(jnp.bfloat16)


def solution(mesh):
    in_specs = (
        P(("group", "ctx"), "exp"),
        P(("group", "ctx"), "exp"),
        P(("group", "ctx"), "exp"),
        P(("group", "ctx", "exp"), None),
        P(),
        P("exp", "group"),
        P(),
        P(),
        P(("group", "ctx", "exp"), None),
        P(("ctx", "exp"), "group", None),
        P(("ctx", "exp"), "group", None),
        P(None, None, "exp"),
        P("exp", None),
    )
    out_specs = P(("group", "ctx", "exp"), None)
    return jax.shard_map(
        on_device, mesh=mesh, in_specs=in_specs, out_specs=out_specs, check_vma=False
    )
```

profile of v0, /device:TPU:0, one launch (start us, length us, event | category | flops | bytes accessed | tf_op | source)
XLA Modules:
  0.0 210.5 jit_solution(2742039219571788179)
XLA Ops:
  6.5 0.7 all-gather.4.cloned.1.call-update
  7.3 0.8 reduce-window.18
  8.1 1.0 copy.36
  9.2 0.7 select_reduce_fusion.1
  10.0 0.1 copy.38
  10.1 2.2 %conditional.2 = (f32[1,3,128]{2,1,0:T(4,128)S(1)}, f32[1,3,128]{2,1,0:T(4,128)S(1)}, f32[1,3,128,128]{3,2,1,0:T(8,128)S(1)}) conditional(s32[]{:T(128)} %convert_element_type.86, () %tuple.50, (s32[]{:T(128)}, s32[128]{0:T(128)S(1)}, s32[128]{0:T(128)S(1)}, bf16[128,1,3,128]{0,3,2,1:T(8,128)(2,1)S(1)}, bf16[128,128]{1,0:T(8,128)(2,1)}, ...), branch_computations={%region_2.3_spmd, %region_3.6_spmd} | conditional | flops 25708544 | bytes 1036328 | solution.py:60
  10.2 0.9 fusion.64
  11.2 1.0 fusion.3
  12.3 0.8 pad_maximum_fusion
  13.0 15.4 %while.24 = (s32[]{:T(128)}, bf16[2,128,128]{2,1,0:T(8,128)(2,1)S(1)}, f32[1,3,128]{2,1,0:T(4,128)S(1)}, f32[1,3,128]{2,1,0:T(4,128)S(1)}, f32[1,3,128,128]{3,2,...) while((s32[]{:T(128)}, ...), condition=%wide.region_11.12_spmd.clone, body=%wide.region_6.11_spmd.clone.sunk | while | flops 25757064 | bytes 1635191 | solution.py:105
  13.0 2.4 %collective-permute-start = (bf16[2,128,128]{2,1,0:T(8,128)(2,1)S(1)}, bf16[2,128,128]{2,1,0:T(8,128)(2,1)S(1)}, u32[]{:S(2)}, u32[]{:S(2)}) collective-permute-start(bf16[2,128,128]{2,1,0:T(8,128)(2,1)S(1)} %get-tuple-element.551), channel_id=1, source_target_pairs={{0,4},{4,8},{8,12},{12,16},{16,20},{20,24},{24,28},{1,5},{5,9},{9,... | collective-permute-start | bytes 196616 | tf_op jit(solution)/shard_map/while/body/eval_jaxpr/ppermute | solution.py:17
  15.5 0.8 collective-permute-done
  16.3 5.7 %collective-permute-start = (bf16[2,128,128]{2,1,0:T(8,128)(2,1)S(1)}, bf16[2,128,128]{2,1,0:T(8,128)(2,1)S(1)}, u32[]{:S(2)}, u32[]{:S(2)}) collective-permute-start(bf16[2,128,128]{2,1,0:T(8,128)(2,1)S(1)} %get-tuple-element.551), channel_id=1, source_target_pairs={{0,4},{4,8},{8,12},{12,16},{16,20},{20,24},{24,28},{1,5},{5,9},{9,... | collective-permute-start | bytes 196616 | tf_op jit(solution)/shard_map/while/body/eval_jaxpr/ppermute | solution.py:17
  22.0 0.8 collective-permute-done
  22.9 4.7 %collective-permute-start = (bf16[2,128,128]{2,1,0:T(8,128)(2,1)S(1)}, bf16[2,128,128]{2,1,0:T(8,128)(2,1)S(1)}, u32[]{:S(2)}, u32[]{:S(2)}) collective-permute-start(bf16[2,128,128]{2,1,0:T(8,128)(2,1)S(1)} %get-tuple-element.551), channel_id=1, source_target_pairs={{0,4},{4,8},{8,12},{12,16},{16,20},{20,24},{24,28},{1,5},{5,9},{9,... | collective-permute-start | bytes 196616 | tf_op jit(solution)/shard_map/while/body/eval_jaxpr/ppermute | solution.py:17
  27.6 0.8 collective-permute-done
  28.5 0.1 copy.39
  28.7 5.8 %all-gather.4.cloned.1.call-done = bf16[384,1536]{1,0:T(8,128)(2,1)} async-done(((bf16[384,768]{1,0:T(8,128)(2,1)}), bf16[384,1536]{1,0:T(8,128)(2,1)}) %all-gather.4.cloned.1.call-update) | async-done | bytes 1179664 | tf_op jit(solution)/shard_map/all_gather | solution.py:109
  34.4 2.4 %convolution_convert_fusion.3 = bf16[128,1536]{1,0:T(8,128)(2,1)} fusion(bf16[128,384]{0,1:T(8,128)(2,1)S(1)} %bitcast.143, bf16[384,1536]{1,0:T(8,128)(2,1)} %all-gather.4.cloned.1.call-done), kind=kOutput, calls=%fused_computation.54 | convolution fusion | flops 151191552 | bytes 1671168 | tf_op jit(solution)/shard_map/dot_general | solution.py:113
  36.9 0.7 all-gather.6.cloned.1.call-update
  37.7 0.1 reshape.273
  37.9 0.6 reduce-window.19
  38.4 0.2 slice_reduce_fusion
  38.8 0.1 reduce_sum.97
  39.0 0.1 fusion.52
  39.1 20.7 %reduce-scatter.3.cloned.1.call-done = bf16[32,1536]{1,0:T(8,128)(2,1)} async-done(((bf16[128,1536]{1,0:T(8,128)(2,1)}), bf16[32,1536]{1,0:T(8,128)(2,1)}) %reduce-scatter.3.cloned.1.call-update) | async-done | bytes 98320 | tf_op jit(solution)/shard_map/reduce_scatter | solution.py:112
  59.8 1.0 fusion.47
  60.8 1.0 fusion.49
  61.8 0.4 convolution_convert_fusion.1
  62.2 1.3 reshape.276
  63.6 3.7 %all-to-all-start = ((bf16[16,18,1536]{2,1,0:T(8,128)(2,1)}), bf16[16,18,1536]{2,1,0:T(8,128)(2,1)S(1)}, u32[]{:S(2)}, u32[]{:S(2)}) async-start(bf16[16,18,1536]{2,1,0:T(8,128)(2,1)} %reshape.276), calls=%async_computation.2 | async-start | bytes 2359296 | tf_op jit(solution)/shard_map/all_to_all | solution.py:169
  67.3 0.5 all-gather.8.cloned.1.call-update
  67.9 0.1 mul.154
  68.0 36.7 %all-gather.6.cloned.1.call-done = bf16[1,1536,1024]{2,1,0:T(8,128)(2,1)} async-done(((bf16[1,768,1024]{2,1,0:T(8,128)(2,1)}), bf16[1,1536,1024]{2,1,0:T(8,128)(2,1)}) %all-gather.6.cloned.1.call-update) | async-done | bytes 3145744 | tf_op jit(solution)/shard_map/all_gather | solution.py:164
  104.7 4.5 %fusion.39 = f32[16,1,18,1024]{3,2,0,1:T(8,128)} fusion(bf16[16,18,1536]{2,1,0:T(8,128)(2,1)S(1)} %all-to-all-done, bf16[1,1536,1024]{2,1,0:T(8,128)(2,1)} %all-gather.6.cloned.1.call-done), kind=kOutput, calls=%fused_computation.59 | convolution fusion | flops 905969664 | bytes 5210112 | tf_op jit(solution)/shard_map/nekd,edf->nekf/dot_general | solution.py:172
  109.2 24.2 %all-gather.8.cloned.1.call-done = bf16[1,1536,512]{2,1,0:T(8,128)(2,1)} async-done(((bf16[1,768,512]{2,1,0:T(8,128)(2,1)}), bf16[1,1536,512]{2,1,0:T(8,128)(2,1)}) %all-gather.8.cloned.1.call-update) | async-done | bytes 1572880 | tf_op jit(solution)/shard_map/all_gather | solution.py:165
  133.4 3.8 %convolution_convert_fusion = bf16[16,18,1536]{2,1,0:T(8,128)(2,1)} fusion(bf16[1,1536,512]{2,1,0:T(8,128)(2,1)} %all-gather.8.cloned.1.call-done, f32[16,1,18,1024]{3,2,0,1:T(8,128)} %fusion.39), kind=kOutput, calls=%fused_computation.51 | convolution fusion | flops 454311936 | bytes 3637248 | tf_op jit(solution)/shard_map/nekf,edf->nekd/dot_general | solution.py:178
  137.2 5.7 %all-to-all-start.1 = ((bf16[16,18,1536]{2,1,0:T(8,128)(2,1)}), bf16[16,18,1536]{2,1,0:T(8,128)(2,1)}, u32[]{:S(2)}, u32[]{:S(2)}) async-start(bf16[16,18,1536]{2,1,0:T(8,128)(2,1)} %convolution_convert_fusion), calls=%async_computation.3 | async-start | bytes 2359296 | tf_op jit(solution)/shard_map/all_to_all | solution.py:181
  142.9 37.6 %all_gather.13 = bf16[128,1536]{1,0:T(8,128)(2,1)S(1)} all-gather(bf16[32,1536]{1,0:T(8,128)(2,1)S(1)} %fusion.49), channel_id=1, replica_groups=mesh['group'=2,'ctx'=4,'exp'=4] {'exp'}, dimensions={0}, use_global_device_ids=true | all-gather | bytes 491520 | tf_op jit(solution)/shard_map/all_gather | solution.py:132
  180.5 0.4 fusion.37
  180.9 1.0 convolution_convert_fusion.2
  182.0 0.1 fusion.66
  182.3 1.5 reshape.280
  183.8 1.1 gather_fusion
  184.9 0.2 gather.7
  185.1 0.9 multiply_reduce_fusion
  186.0 16.4 %reduce-scatter.5.cloned.1.call-done = bf16[32,1536]{1,0:T(8,128)(2,1)} async-done(((bf16[128,1536]{1,0:T(8,128)(2,1)}), bf16[32,1536]{1,0:T(8,128)(2,1)}) %reduce-scatter.5.cloned.1.call-update) | async-done | bytes 98320 | tf_op jit(solution)/shard_map/reduce_scatter | solution.py:138
  202.4 1.6 fusion.51
  (56 shorter events, 1.0 us)
Async XLA Ops:
  6.5 174.0 %copy-start = (bf16[1536,2,256]{2,1,0:T(2,128)(2,1)S(1)}, bf16[1536,2,256]{2,1,0:T(2,128)(2,1)}, u32[]{:S(2)}) copy-start(bf16[1536,2,256]{2,1,0:T(2,128)(2,1)} %param.30) | copy-start | bytes 4718596
  6.5 27.9 %all-gather.4.cloned.1.call-start = ((), (), s32[]{:S(2)}) async-start(), calls=%async_computation.4 | async-start | bytes 1769472 | tf_op jit(solution)/shard_map/all_gather | solution.py:109
  7.3 52.5 %reduce-scatter.3.cloned.1.call-start = ((), (), s32[]{:S(2)}) async-start(), calls=%async_computation.5 | async-start | bytes 491520 | tf_op jit(solution)/shard_map/reduce_scatter | solution.py:112
  13.0 3.2 %collective-permute-start = (bf16[2,128,128]{2,1,0:T(8,128)(2,1)S(1)}, bf16[2,128,128]{2,1,0:T(8,128)(2,1)S(1)}, u32[]{:S(2)}, u32[]{:S(2)}) collective-permute-start(bf16[2,128,128]{2,1,0:T(8,128)(2,1)S(1)} %get-tuple-element.551), channel_id=1, source_target_pairs={{0,4},{4,8},{8,12},{12,16},{16,20},{20,24},{24,28},{1,5},{5,9},{9,... | collective-permute-start | bytes 196616 | tf_op jit(solution)/shard_map/while/body/eval_jaxpr/ppermute | solution.py:17
  16.3 6.5 %collective-permute-start = (bf16[2,128,128]{2,1,0:T(8,128)(2,1)S(1)}, bf16[2,128,128]{2,1,0:T(8,128)(2,1)S(1)}, u32[]{:S(2)}, u32[]{:S(2)}) collective-permute-start(bf16[2,128,128]{2,1,0:T(8,128)(2,1)S(1)} %get-tuple-element.551), channel_id=1, source_target_pairs={{0,4},{4,8},{8,12},{12,16},{16,20},{20,24},{24,28},{1,5},{5,9},{9,... | collective-permute-start | bytes 196616 | tf_op jit(solution)/shard_map/while/body/eval_jaxpr/ppermute | solution.py:17
  22.9 5.6 %collective-permute-start = (bf16[2,128,128]{2,1,0:T(8,128)(2,1)S(1)}, bf16[2,128,128]{2,1,0:T(8,128)(2,1)S(1)}, u32[]{:S(2)}, u32[]{:S(2)}) collective-permute-start(bf16[2,128,128]{2,1,0:T(8,128)(2,1)S(1)} %get-tuple-element.551), channel_id=1, source_target_pairs={{0,4},{4,8},{8,12},{12,16},{16,20},{20,24},{24,28},{1,5},{5,9},{9,... | collective-permute-start | bytes 196616 | tf_op jit(solution)/shard_map/while/body/eval_jaxpr/ppermute | solution.py:17
  34.4 3.2 %copy-start.4 = (s32[32,6]{0,1:T(8,128)S(1)}, s32[32,6]{0,1:T(8,128)}, u32[]{:S(2)}) copy-start(s32[32,6]{0,1:T(8,128)} %param.27) | copy-start | bytes 2308
  34.4 25.4 %copy-start.1 = (bf16[32,1536]{1,0:T(8,128)(2,1)S(1)}, bf16[32,1536]{1,0:T(8,128)(2,1)}, u32[]{:S(2)}) copy-start(bf16[32,1536]{1,0:T(8,128)(2,1)} %param.22) | copy-start | bytes 294916
  36.9 24.0 %copy-start.5 = (f32[1536]{0:T(1024)S(1)}, f32[1536]{0:T(1024)}, u32[]{:S(2)}) copy-start(f32[1536]{0:T(1024)} %param.25) | copy-start | bytes 18436
  36.9 67.8 %all-gather.6.cloned.1.call-start = ((), (), s32[]{:S(2)}) async-start(), calls=%async_computation.7 | async-start | bytes 4718592 | tf_op jit(solution)/shard_map/all_gather | solution.py:164
  63.6 41.1 %all-to-all-start = ((bf16[16,18,1536]{2,1,0:T(8,128)(2,1)}), bf16[16,18,1536]{2,1,0:T(8,128)(2,1)S(1)}, u32[]{:S(2)}, u32[]{:S(2)}) async-start(bf16[16,18,1536]{2,1,0:T(8,128)(2,1)} %reshape.276), calls=%async_computation.2 | async-start | bytes 2359296 | tf_op jit(solution)/shard_map/all_to_all | solution.py:169
  67.3 66.1 %all-gather.8.cloned.1.call-start = ((), (), s32[]{:S(2)}) async-start(), calls=%async_computation.8 | async-start | bytes 2359296 | tf_op jit(solution)/shard_map/all_gather | solution.py:165
  137.2 45.1 %all-to-all-start.1 = ((bf16[16,18,1536]{2,1,0:T(8,128)(2,1)}), bf16[16,18,1536]{2,1,0:T(8,128)(2,1)}, u32[]{:S(2)}, u32[]{:S(2)}) async-start(bf16[16,18,1536]{2,1,0:T(8,128)(2,1)} %convolution_convert_fusion), calls=%async_computation.3 | async-start | bytes 2359296 | tf_op jit(solution)/shard_map/all_to_all | solution.py:181
  142.8 38.1 %copy-start.6 = (bf16[256,1536]{1,0:T(8,128)(2,1)S(1)}, bf16[256,1536]{1,0:T(8,128)(2,1)}, u32[]{:S(2)}) copy-start(bf16[256,1536]{1,0:T(8,128)(2,1)} %param.31) | copy-start | bytes 2359300
  142.8 59.6 %reduce-scatter.5.cloned.1.call-start = ((), (), s32[]{:S(2)}) async-start(), calls=%async_computation.6 | async-start | bytes 491520 | tf_op jit(solution)/shard_map/reduce_scatter | solution.py:138
  180.5 1.5 copy-start.3
  184.9 17.5 %copy-start.2 = (bf16[32,1536]{1,0:T(8,128)(2,1)S(1)}, bf16[32,1536]{1,0:T(8,128)(2,1)}, u32[]{:S(2)}) copy-start(bf16[32,1536]{1,0:T(8,128)(2,1)} %reduce-scatter.3.cloned.1.call-done) | copy-start | bytes 294916
Sparse Core Ops, SparseCore 0:
  8.9 25.4 all-gather.3
  37.0 22.7 reduce-scatter.2
  61.4 43.2 all-gather.5
  106.1 27.1 all-gather.7
  182.1 20.2 reduce-scatter.4
where the time goes:
time: 212 us; the launch traced here: 211 us
  waiting for transfers between devices  108 us (51%)
  blocking collectives  37.6 us (18%)
  starting transfers between devices  22.2 us (10%)
  matrix products  14.6 us (7%)
  between operations  13.4 us (6%)
  other arithmetic  8.04 us (4%)
  local copies, waits for them, and re-layouts  6.15 us (3%)
    all_gather x1, blocking collectives, on_device(): all_normed = lax.all_gather(normed, 'exp', axis=0, tiled=True)  37.6 us
    all_gather x1, waiting for transfers between devices, on_device(): lax.all_gather(expert_gate_up, 'group', axis=1, tiled=True)  36.7 us
    all_gather x1, waiting for transfers between devices, on_device(): lax.all_gather(expert_down, 'group', axis=1, tiled=True)  24.2 us
    reduce_scatter x1, waiting for transfers between devices, on_device(): lax.psum_scatter(jnp.dot(picked, out_full, preferred_element_type=jnp.flo...  20.7 us
    reduce_scatter x1, waiting for transfers between devices, on_device(): lax.psum_scatter(jnp.dot(picked, shared_down, preferred_element_type=jnp....  16.4 us
    ppermute x3, starting transfers between devices, passed_along(): return lax.ppermute(shard, axis, pairs)  12.7 us
    all_gather x1, waiting for transfers between devices, on_device(): out_full = lax.all_gather(w_out, 'group', axis=1, tiled=True)  5.76 us
    all_to_all x1, starting transfers between devices, on_device(): lax.all_to_all(result.reshape(arrived.shape), ('ctx', 'exp'), split_axis=...  5.66 us
  transfers between devices with their start and end apart: 10, of which 8 were waited for; matrix products, arithmetic and copies ran while one was open for 10% of the time, Pallas kernels for 0%

commit v1 on v0

--- a/solution.py
+++ b/solution.py
@@ -18,7 +18,9 @@
 
 
 def doc_starts(positions, doc_lengths):
-    doc_ends = jnp.cumsum(doc_lengths, dtype=jnp.int32)
+    order = jnp.arange(doc_lengths.shape[0], dtype=jnp.int32)
+    before = (order[None, :] <= order[:, None]).astype(jnp.int32)
+    doc_ends = jnp.sum(before * doc_lengths[None, :], axis=1, dtype=jnp.int32)
     passed = (doc_ends[None, :] <= positions[:, None]).astype(jnp.int32)
     return jnp.sum(passed * doc_lengths[None, :], axis=1, dtype=jnp.int32)
 
@@ -58,6 +60,53 @@
         return inner_state
 
     return lax.cond(useful, run_block, keep_block, soft_state)
+
+
+def turned(shard, axis, by):
+    length = lax.axis_size(axis)
+    return lax.ppermute(shard, axis, [(i, (i + by) % length) for i in range(length)])
+
+
+def swapped(shard):
+    return lax.ppermute(shard, "group", [(0, 1), (1, 0)])
+
+
+def matmul(rows, weights):
+    return jnp.dot(rows, weights, preferred_element_type=jnp.float32).astype(jnp.bfloat16)
+
+
+def joined(own_first, own, other):
+    first = jnp.where(own_first, own, other)
+    second = jnp.where(own_first, other, own)
+    return jnp.concatenate([first, second], axis=-1)
+
+
+def summed_from(partial, length, rows, step):
+    total = partial[:rows].astype(jnp.float32)
+    for by in range(1, length):
+        piece = partial[by * rows : (by + 1) * rows]
+        total = total + turned(piece, "exp", step * by).astype(jnp.float32)
+    return total
+
+
+def attend_window(kv, first_key, query_heads, query_pos, query_start):
+    count = kv.shape[1]
+    key_pos = first_key + jnp.arange(count, dtype=jnp.int32)
+    allowed = (key_pos[None, :] <= query_pos[:, None]) & (key_pos[None, :] >= query_start[:, None])
+    key_heads = kv[0].reshape(count, -1, HEAD)
+    value_heads = kv[1].reshape(count, -1, HEAD)
+    scores = jnp.einsum(
+        "tgpd,sgd->gpts", query_heads, key_heads, preferred_element_type=jnp.float32
+    ) * (1.0 / math.sqrt(HEAD))
+    scores = jnp.where(allowed, scores, neg_big)
+    weights = jnp.where(allowed, jnp.exp(scores - jnp.max(scores, axis=-1, keepdims=True)), 0.0)
+    acc = jnp.einsum(
+        "gpts,sgd->gptd",
+        weights.astype(jnp.bfloat16),
+        value_heads,
+        preferred_element_type=jnp.float32,
+    )
+    return acc / jnp.sum(weights, axis=-1, keepdims=True)
 
 
 def on_device(
@@ -89,32 +138,49 @@
         jnp.zeros((kv_count, per_kv, rows_dev), jnp.float32),
         jnp.zeros((kv_count, per_kv, rows_dev, HEAD), jnp.float32),
     )
+    group_size = lax.axis_size("group")
+    swap = group_size == 2
     kv_own = jnp.stack([keys, values])
-    soft_state = visit_block(init_state, kv_own, my_block, query_heads, query_pos, query_start)
-
-    def cycle_turn(turn_idx, loop_state):
-        moving, inner_state = loop_state
-        moving = passed_along(moving, ("group", "ctx"), 1)
-        return (
-            moving,
-            visit_block(
-                inner_state, moving, my_block - turn_idx, query_heads, query_pos, query_start
-            ),
+    if look_back <= 8:
+        blocks = [passed_along(kv_own, ("group", "ctx"), by) for by in range(look_back - 1, 0, -1)]
+        kv_all = jnp.concatenate([*blocks, kv_own], axis=1)
+    if swap:
+        out_other, gate_other, down_other = (
+            swapped(w_out), swapped(expert_gate_up), swapped(expert_down)
         )
-
-    moving, soft_state = lax.fori_loop(1, look_back, cycle_turn, (kv_own, soft_state))
-    run_max, run_sum, run_acc = soft_state
-    attended = run_acc / run_sum[..., None]
+        own_first = lax.axis_index("group") == 0
+    if look_back <= 8:
+        first_key = (my_block - (look_back - 1)) * rows_dev
+        attended = attend_window(kv_all, first_key, query_heads, query_pos, query_start)
+    else:
+        soft_state = visit_block(init_state, kv_own, my_block, query_heads, query_pos, query_start)
+
+        def cycle_turn(turn_idx, loop_state):
+            moving, inner_state = loop_state
+            moving = passed_along(moving, ("group", "ctx"), 1)
+            return (
+                moving,
+                visit_block(
+                    inner_state, moving, my_block - turn_idx, query_heads, query_pos, query_start
+                ),
+            )
+
+        moving, soft_state = lax.fori_loop(1, look_back, cycle_turn, (kv_own, soft_state))
+        run_max, run_sum, run_acc = soft_state
+        attended = run_acc / run_sum[..., None]
     attended = jnp.transpose(attended, (2, 0, 1, 3)).reshape(rows_dev, -1).astype(jnp.bfloat16)
-    out_full = lax.all_gather(w_out, "group", axis=1, tiled=True)
-    tok_e = rows_dev // lax.axis_size("exp")
-    picked = attended
-    projected = lax.psum_scatter(
-        jnp.dot(picked, out_full, preferred_element_type=jnp.float32).astype(jnp.bfloat16),
-        "exp",
-        scatter_dimension=0,
-        tiled=True,
-    ).astype(jnp.float32)
+    exp_size = lax.axis_size("exp")
+    exp_me = lax.axis_index("exp")
+    tok_e = rows_dev // exp_size
+    ahead = [(exp_me + by) % exp_size for by in range(exp_size)]
+    rolled = jnp.concatenate(
+        [lax.dynamic_slice_in_dim(attended, to * tok_e, tok_e, 0) for to in ahead], axis=0
+    )
+    if swap:
+        partial = joined(own_first, matmul(rolled, w_out), matmul(rolled, out_other))
+    else:
+        partial = matmul(rolled, lax.all_gather(w_out, "group", axis=1, tiled=True))
+    projected = summed_from(partial, exp_size, tok_e, 1)
     stream = (residual_in.astype(jnp.float32) + projected).astype(jnp.bfloat16)
     stream_f = stream.astype(jnp.float32)
     normed = (
@@ -129,26 +195,19 @@
     picked_logits = jnp.sum(jnp.where(chosen, logits[:, None, :], 0.0), axis=-1)
     raw_gates = jax.nn.sigmoid(picked_logits)
     gate_probs = raw_gates / jnp.sum(raw_gates, axis=-1, keepdims=True)
-    all_normed = lax.all_gather(normed, "exp", axis=0, tiled=True)
+    all_normed = jnp.concatenate(
+        [normed, *[turned(normed, "exp", by) for by in range(1, exp_size)]], axis=0
+    )
     shared_pre = jnp.einsum(
         "td,dkf->tkf", all_normed, shared_gate_up, preferred_element_type=jnp.float32
     )
     shared_act = (jax.nn.silu(shared_pre[:, 0]) * shared_pre[:, 1]).astype(jnp.bfloat16)
-    picked = shared_act
-    shared_out = lax.psum_scatter(
-        jnp.dot(picked, shared_down, preferred_element_type=jnp.float32).astype(jnp.bfloat16),
-        "exp",
-        scatter_dimension=0,
-        tiled=True,
-    ).astype(jnp.float32)
+    shared_out = summed_from(matmul(shared_act, shared_down), exp_size, tok_e, -1)
     slot_count = max(2, 3 * tok_e * route_count // (2 * expert_count))
     flat_ids = expert_ids.reshape(-1)
-    one_hot = (flat_ids[:, None] == jnp.arange(expert_count, dtype=jnp.int32)[None, :]).astype(
-        jnp.int32
-    )
-    slot_of = jnp.sum(
-        (jnp.cumsum(one_hot, axis=0, dtype=jnp.int32) - 1) * one_hot, axis=1, dtype=jnp.int32
-    )
+    order = jnp.arange(flat_ids.shape[0], dtype=jnp.int32)
+    earlier = (flat_ids[None, :] == flat_ids[:, None]) & (order[None, :] < order[:, None])
+    slot_of = jnp.sum(earlier.astype(jnp.int32), axis=1, dtype=jnp.int32)
     target = flat_ids * slot_count + slot_of
     placing = (
         jnp.arange(expert_count * slot_count, dtype=jnp.int32)[:, None] == target[None, :]
@@ -160,24 +219,37 @@
         .astype(jnp.bfloat16)
         .reshape(expert_count, slot_count, model_width)
     )
-    gate_up_full, down_full = (
-        lax.all_gather(expert_gate_up, "group", axis=1, tiled=True),
-        lax.all_gather(expert_down, "group", axis=1, tiled=True),
-    )
-    hidden_count = down_full.shape[2]
-    local_experts = gate_up_full.shape[0]
+    if not swap:
+        gate_up_full = lax.all_gather(expert_gate_up, "group", axis=1, tiled=True)
+        down_full = lax.all_gather(expert_down, "group", axis=1, tiled=True)
+    hidden_count = expert_down.shape[2]
+    local_experts = expert_gate_up.shape[0]
     arrived = lax.all_to_all(outgoing, ("ctx", "exp"), split_axis=0, concat_axis=0, tiled=True)
     sources = arrived.shape[0] // local_experts
     grouped = arrived.reshape(sources, local_experts, arrived.shape[1], arrived.shape[2])
-    pre_act = jnp.einsum(
-        "nekd,edf->nekf", grouped, gate_up_full, preferred_element_type=jnp.float32
-    )
+    if swap:
+        half = model_width // 2
+        mine = lax.dynamic_slice_in_dim(grouped, lax.axis_index("group") * half, half, 3)
+        others = lax.dynamic_slice_in_dim(grouped, (1 - lax.axis_index("group")) * half, half, 3)
+        pre_act = jnp.einsum(
+            "nekd,edf->nekf", mine, expert_gate_up, preferred_element_type=jnp.float32
+        ) + jnp.einsum("nekd,edf->nekf", others, gate_other, preferred_element_type=jnp.float32)
+    else:
+        pre_act = jnp.einsum(
+            "nekd,edf->nekf", grouped, gate_up_full, preferred_element_type=jnp.float32
+        )
     activated = (jax.nn.silu(pre_act[..., :hidden_count]) * pre_act[..., hidden_count:]).astype(
         jnp.bfloat16
     )
-    result = jnp.einsum(
-        "nekf,edf->nekd", activated, down_full, preferred_element_type=jnp.float32
-    ).astype(jnp.bfloat16)
+    def down(rows):
+        return jnp.einsum(
+            "nekf,edf->nekd", activated, rows, preferred_element_type=jnp.float32
+        ).astype(jnp.bfloat16)
+
+    if swap:
+        result = joined(own_first, down(expert_down), down(down_other))
+    else:
+        result = down(down_full)
     returned = lax.all_to_all(
         result.reshape(arrived.shape), ("ctx", "exp"), split_axis=0, concat_axis=0, tiled=True
     )

time: 212 us -> 149 us (0.70)
  blocking collectives: 37.6 us -> 0 us
  waiting for transfers between devices: 108 us -> 80.2 us
  starting transfers between devices: 22.2 us -> 39 us
  between operations: 13.4 us -> 0.43 us
  matrix products: 14.6 us -> 8.89 us
  local copies, waits for them, and re-layouts: 6.15 us -> 9.34 us
  other arithmetic: 8.04 us -> 10.2 us
    all_gather x3 -> x0, waiting for transfers between devices: 66.7 us -> none  [the longest x1 36.7 us: on_device(): lax.all_gather(expert_gate_up, 'group', axis=1, tiled=True)]
    all_gather x1 -> x0, blocking collectives: 37.6 us -> none  [on_device(): all_normed = lax.all_gather(normed, 'exp', axis=0, tiled=True)]
    reduce_scatter x2 -> x0, waiting for transfers between devices: 37.1 us -> none  [the longest x1 20.7 us: on_device(): lax.psum_scatter(jnp.dot(picked, out_full, preferred_element_type=jnp.flo...]
    ppermute x0 -> x12, waiting for transfers between devices: none -> 27.9 us  [the longest x3 21.3 us: swapped(): return lax.ppermute(shard, 'group', [(0, 1), (1, 0)])]
    all_to_all x1, waiting for transfers between devices: 0.01 us -> 26.4 us  [on_device(): lax.all_to_all(outgoing, ('ctx', 'exp'), split_axis=0, concat_axis=0, til...]
    all_to_all x1, waiting for transfers between devices: 0.01 us -> 25.9 us  [on_device(): lax.all_to_all(result.reshape(arrived.shape), ('ctx', 'exp'), split_axis=...]
    ppermute x0 -> x12, starting transfers between devices: none -> 17.3 us  [the longest x9 15.2 us: turned(): lax.ppermute(shard, axis, [(i, (i + by) % length) for i in range(length)])]
    dot_general x6 -> x9, matrix products: 13.6 us -> 7.97 us  [the longest x1 2.21 us: on_device(): jnp.einsum('nekd,edf->nekf', others, gate_other, preferred_element_type=j...]
  transfers between devices with their start and end apart: 10 -> 17, of which waited for: 8 -> 7; matrix products, arithmetic and copies ran while one was open for 10% -> 15% of each run, Pallas kernels for 0% -> 0%
where the time goes in v1:
time: 149 us; the launch traced here: 148 us
  waiting for transfers between devices  80.2 us (54%)
  starting transfers between devices  39 us (26%)
  other arithmetic  10.2 us (7%)
  local copies, waits for them, and re-layouts  9.34 us (6%)
  matrix products  8.89 us (6%)
    all_to_all x1, waiting for transfers between devices, on_device(): lax.all_to_all(outgoing, ('ctx', 'exp'), split_axis=0, concat_axis=0, til...  26.4 us
    all_to_all x1, waiting for transfers between devices, on_device(): lax.all_to_all(result.reshape(arrived.shape), ('ctx', 'exp'), split_axis=...  25.9 us
    ppermute x3, waiting for transfers between devices, swapped(): return lax.ppermute(shard, 'group', [(0, 1), (1, 0)])  21.3 us
    ppermute x9, starting transfers between devices, turned(): lax.ppermute(shard, axis, [(i, (i + by) % length) for i in range(length)])  15.2 us
    ppermute x3, starting transfers between devices, passed_along(): return lax.ppermute(shard, axis, pairs)  11.1 us
    ppermute x9, waiting for transfers between devices, turned(): lax.ppermute(shard, axis, [(i, (i + by) % length) for i in range(length)])  6.64 us
    all_to_all x1, starting transfers between devices, on_device(): lax.all_to_all(result.reshape(arrived.shape), ('ctx', 'exp'), split_axis=...  5.92 us
    all_to_all x1, starting transfers between devices, on_device(): lax.all_to_all(outgoing, ('ctx', 'exp'), split_axis=0, concat_axis=0, til...  4.72 us
  transfers between devices with their start and end apart: 17, of which 7 were waited for; matrix products, arithmetic and copies ran while one was open for 15% of the time, Pallas kernels for 0%

profile of v1, /device:TPU:0, one launch (start us, length us, event | category | flops | bytes accessed | tf_op | source)
XLA Modules:
  0.0 148.1 jit_solution(8046579092838463045)
XLA Ops:
  0.0 0.9 pad_maximum_fusion.2
  0.9 2.3 %collective-permute-start.2 = (bf16[2,128,128]{2,1,0:T(8,128)(2,1)S(1)}, bf16[2,128,128]{2,1,0:T(8,128)(2,1)S(1)}, u32[]{:S(2)}, u32[]{:S(2)}) collective-permute-start(bf16[2,128,128]{2,1,0:T(8,128)(2,1)S(1)} %pad_maximum_fusion.2), channel_id=1, source_target_pairs={{0,4},{4,8},{8,12},{12,16},{16,20},{20,24},{24,28},{1,5},{5,9},{9,... | collective-permute-start | bytes 196616 | tf_op jit(solution)/shard_map/ppermute | solution.py:17
  3.3 4.4 %collective-permute-start.1 = (bf16[2,128,128]{2,1,0:T(8,128)(2,1)S(1)}, bf16[2,128,128]{2,1,0:T(8,128)(2,1)S(1)}, u32[]{:S(2)}, u32[]{:S(2)}) collective-permute-start(bf16[2,128,128]{2,1,0:T(8,128)(2,1)S(1)} %pad_maximum_fusion.2), channel_id=1, source_target_pairs={{0,8},{4,12},{8,16},{12,20},{16,24},{20,28},{1,9},{5,13},{9,17},{1... | collective-permute-start | bytes 196616 | tf_op jit(solution)/shard_map/ppermute | solution.py:17
  7.7 4.3 %collective-permute-start = (bf16[2,128,128]{2,1,0:T(8,128)(2,1)S(1)}, bf16[2,128,128]{2,1,0:T(8,128)(2,1)S(1)}, u32[]{:S(2)}, u32[]{:S(2)}) collective-permute-start(bf16[2,128,128]{2,1,0:T(8,128)(2,1)S(1)} %pad_maximum_fusion.2), channel_id=1, source_target_pairs={{0,12},{4,16},{8,20},{12,24},{16,28},{1,13},{5,17},{9,21},{13,25},... | collective-permute-start | bytes 196616 | tf_op jit(solution)/shard_map/ppermute | solution.py:17
  12.1 0.8 copy.37
  13.3 0.8 select_reduce_fusion.2
  14.1 0.7 select_reduce_fusion.1
  14.9 0.6 compare_and_fusion.1
  15.6 1.0 copy.31
  16.7 0.8 maximum_maximum_fusion
  17.9 0.3 fusion.10
  18.6 0.4 copy-done.2
  19.0 0.3 convolution_convert_fusion.5
  19.3 7.4 %collective-permute-done.3 = bf16[384,768]{1,0:T(8,128)(2,1)S(1)} collective-permute-done((bf16[384,768]{1,0:T(8,128)(2,1)}, bf16[384,768]{1,0:T(8,128)(2,1)S(1)}, u32[]{:S(2)}, u32[]{:S(2)}) %collective-permute-start.3) | collective-permute-done | bytes 589856 | tf_op jit(solution)/shard_map/ppermute | solution.py:71
  26.7 0.3 broadcast_select_fusion.1
  27.1 3.7 %collective-permute-start.6 = (bf16[32,1536]{1,0:T(8,128)(2,1)S(1)}, bf16[32,1536]{1,0:T(8,128)(2,1)S(1)}, u32[]{:S(2)}, u32[]{:S(2)}) collective-permute-start(bf16[32,1536]{1,0:T(8,128)(2,1)S(1)} %get-tuple-element.15), channel_id=1, source_target_pairs={{0,3},{1,0},{2,1},{3,2},{4,7},{5,4},{6,5},{7,6},{8,11},{9,8},{10,9... | collective-permute-start | bytes 294920 | tf_op jit(solution)/shard_map/ppermute | solution.py:67
  30.7 1.0 collective-permute-start.4
  31.8 1.5 %collective-permute-done.6 = bf16[32,1536]{1,0:T(8,128)(2,1)S(1)} collective-permute-done((bf16[32,1536]{1,0:T(8,128)(2,1)S(1)}, bf16[32,1536]{1,0:T(8,128)(2,1)S(1)}, u32[]{:S(2)}, u32[]{:S(2)}) %collective-permute-start.6) | collective-permute-done | bytes 98336 | tf_op jit(solution)/shard_map/ppermute | solution.py:67
  33.4 5.1 %collective-permute-done.5 = bf16[32,1536]{1,0:T(8,128)(2,1)S(1)} collective-permute-done((bf16[32,1536]{1,0:T(8,128)(2,1)S(1)}, bf16[32,1536]{1,0:T(8,128)(2,1)S(1)}, u32[]{:S(2)}, u32[]{:S(2)}) %collective-permute-start.5) | collective-permute-done | bytes 98336 | tf_op jit(solution)/shard_map/ppermute | solution.py:67
  38.8 0.4 convolution_convert_fusion
  39.2 1.3 reshape.190
  40.5 4.7 %all-to-all-start = ((bf16[16,18,1536]{2,1,0:T(8,128)(2,1)}), bf16[16,18,1536]{2,1,0:T(8,128)(2,1)S(1)}, u32[]{:S(2)}, u32[]{:S(2)}) async-start(bf16[16,18,1536]{2,1,0:T(8,128)(2,1)} %reshape.190), calls=%async_computation | async-start | bytes 2359296 | tf_op jit(solution)/shard_map/all_to_all | solution.py:227
  45.2 1.8 %collective-permute-start.13 = (bf16[1,768,1024]{2,1,0:T(8,128)(2,1)}, bf16[1,768,1024]{2,1,0:T(8,128)(2,1)}, u32[]{:S(2)}, u32[]{:S(2)}) collective-permute-start(bf16[1,768,1024]{2,1,0:T(8,128)(2,1)} %param.22), channel_id=1, source_target_pairs={{0,16},{16,0},{1,17},{17,1},{2,18},{18,2},{3,19},{19,3},{4,20},{20... | collective-permute-start | bytes 4718600 | tf_op jit(solution)/shard_map/ppermute | solution.py:71
  47.0 0.3 collective-permute-start.14
  47.4 0.6 pad_clamp_fusion
  48.0 3.7 %collective-permute-start.9 = (bf16[32,1536]{1,0:T(8,128)(2,1)S(1)}, bf16[32,1536]{1,0:T(8,128)(2,1)S(1)}, u32[]{:S(2)}, u32[]{:S(2)}) collective-permute-start(bf16[32,1536]{1,0:T(8,128)(2,1)S(1)} %fusion.34), channel_id=1, source_target_pairs={{0,3},{1,0},{2,1},{3,2},{4,7},{5,4},{6,5},{7,6},{8,11},{9,8},{10,9... | collective-permute-start | bytes 294920 | tf_op jit(solution)/shard_map/ppermute | solution.py:67
  51.7 1.1 collective-permute-start.7
  52.8 26.4 %all-to-all-done = bf16[16,18,1536]{2,1,0:T(8,128)(2,1)S(1)} async-done(((bf16[16,18,1536]{2,1,0:T(8,128)(2,1)}), bf16[16,18,1536]{2,1,0:T(8,128)(2,1)S(1)}, u32[]{:S(2)}, u32[]{:S(2)}) %all-to-all-start) | async-done | bytes 884768 | tf_op jit(solution)/shard_map/all_to_all | solution.py:227
  79.2 2.2 %fusion.2 = f32[16,18,1024]{2,1,0:T(8,128)S(1)} fusion(bf16[1,768,1024]{2,1,0:T(8,128)(2,1)} %param.22, bf16[16,18,1536]{2,1,0:T(8,128)(2,1)S(1)} %all-to-all-done, s32[]{:T(128)S(6)} %select_n.128), kind=kOutput, calls=%fused_computation.5 | convolution fusion | flops 452984832 | bytes 3342340 | tf_op jit(solution)/shard_map/nekd,edf->nekf/dot_general | solution.py:234
  81.4 1.4 collective-permute-done.13
  82.8 2.2 %add_bitcast_fusion = f32[16,1,18,1024]{3,2,0,1:T(8,128)S(1)} fusion(f32[16,18,1024]{2,1,0:T(8,128)S(1)} %fusion.2, bf16[1,768,1024]{2,1,0:T(8,128)(2,1)} %collective-permute-done.13, bf16[16,18,1536]{2,1,0:T(8,128)(2,1)S(1)} %all-to-all-done, s32[]{:T(128)S(6)} %select_n.129), kind=kOutput, calls=%fused_computation.10 | convolution fusion | flops 453279744 | bytes 4915204 | tf_op jit(solution)/shard_map/nekd,edf->nekf/dot_general | solution.py:236
  85.3 0.9 copy-done.1
  86.1 0.5 convolution_convert_fusion.3
  86.7 12.4 %collective-permute-done.14 = bf16[1,768,512]{2,1,0:T(8,128)(2,1)} collective-permute-done((bf16[1,768,512]{2,1,0:T(8,128)(2,1)}, bf16[1,768,512]{2,1,0:T(8,128)(2,1)}, u32[]{:S(2)}, u32[]{:S(2)}) %collective-permute-start.14) | collective-permute-done | bytes 786464 | tf_op jit(solution)/shard_map/ppermute | solution.py:71
  99.1 1.6 %select_bitcast_fusion.1 = (bf16[16,1,18,768]{3,2,0,1:T(8,128)(2,1)S(1)}, bf16[16,1,18,768]{3,2,0,1:T(8,128)(2,1)S(1)}) fusion(bf16[16,18,768]{2,1,0:T(8,128)(2,1)S(1)} %convolution_convert_fusion.3, pred[]{:T(512)S(6)} %eq.48, bf16[1,768,512]{2,1,0:T(8,128)(2,1)} %collective-permute-done.14, bf16[16,1,18,512]{3,2,0,1:T(8,128)(2,1)S(1)} %fusion.11), kind=kOutput, calls=%fused_computation.29 | convolution fusion | flops 227155968 | bytes 2408449 | tf_op jit(solution)/shard_map/nekf,edf->nekd/dot_general | solution.py:245
  100.7 1.1 maximum_bitcast_fusion
  101.8 5.9 %all-to-all-start.1 = ((bf16[16,18,1536]{2,1,0:T(8,128)(2,1)}), bf16[16,18,1536]{2,1,0:T(8,128)(2,1)}, u32[]{:S(2)}, u32[]{:S(2)}) async-start(bf16[16,18,1536]{2,1,0:T(8,128)(2,1)} %maximum_bitcast_fusion), calls=%async_computation.1 | async-start | bytes 2359296 | tf_op jit(solution)/shard_map/all_to_all | solution.py:253
  108.1 0.4 fusion.4
  108.5 0.7 copy-done.7
  109.5 0.7 fusion.53
  110.2 1.9 %collective-permute-start.12 = (bf16[32,1536]{1,0:T(8,128)(2,1)}, bf16[32,1536]{1,0:T(8,128)(2,1)}, u32[]{:S(2)}, u32[]{:S(2)}) collective-permute-start(bf16[32,1536]{1,0:T(8,128)(2,1)} %get-tuple-element.12), channel_id=1, source_target_pairs={{0,1},{1,2},{2,3},{3,0},{4,5},{5,6},{6,7},{7,4},{8,9},{9,10},{10,1... | collective-permute-start | bytes 294920 | tf_op jit(solution)/shard_map/ppermute | solution.py:67
  112.1 2.4 %collective-permute-start.11 = (bf16[32,1536]{1,0:T(8,128)(2,1)}, bf16[32,1536]{1,0:T(8,128)(2,1)}, u32[]{:S(2)}, u32[]{:S(2)}) collective-permute-start(bf16[32,1536]{1,0:T(8,128)(2,1)} %get-tuple-element.13), channel_id=1, source_target_pairs={{0,2},{1,3},{2,0},{3,1},{4,6},{5,7},{6,4},{7,5},{8,10},{9,11},{10,... | collective-permute-start | bytes 294920 | tf_op jit(solution)/shard_map/ppermute | solution.py:67
  114.5 1.5 collective-permute-start.10
  115.9 25.9 %all-to-all-done.1 = bf16[16,18,1536]{2,1,0:T(8,128)(2,1)} async-done(((bf16[16,18,1536]{2,1,0:T(8,128)(2,1)}), bf16[16,18,1536]{2,1,0:T(8,128)(2,1)}, u32[]{:S(2)}, u32[]{:S(2)}) %all-to-all-start.1) | async-done | bytes 884768 | tf_op jit(solution)/shard_map/all_to_all | solution.py:253
  141.8 1.5 %reshape.197 = bf16[288,1536]{1,0:T(8,128)(2,1)S(1)} reshape(bf16[16,18,1536]{2,1,0:T(8,128)(2,1)} %all-to-all-done.1) | data formatting | bytes 1769472 | tf_op jit(solution)/shard_map/reshape | solution.py:256
  143.3 1.2 gather_fusion
  144.7 1.6 %multiply_reduce_fusion = f32[32,1536]{1,0:T(8,128)S(1)} fusion(bf16[32,6,1536]{2,1,0:T(8,128)(2,1)S(1)} %gather.7, f32[32,6]{1,0:T(8,128)S(1)} %copy.36, pred[32,6]{1,0:T(8,128)(4,1)} %get-tuple-element.5), kind=kLoop, calls=%fused_computation.9 | loop fusion | flops 1130496 | bytes 787392 | tf_op jit(solution)/shard_map/reduce_sum | solution.py:262
  146.4 1.7 %fusion.36 = bf16[32,1536]{1,0:T(8,128)(2,1)} fusion(f32[32,1536]{1,0:T(8,128)S(1)} %multiply_reduce_fusion, bf16[32,1536]{1,0:T(8,128)(2,1)S(1)} %get-tuple-element.8, bf16[32,1536]{1,0:T(8,128)(2,1)} %collective-permute-done.12, bf16[32,1536]{1,0:T(8,128)(2,1)} %collective-permute-done.11, bf16[32,1536]{1,0:T(8,128)(2,1)} %collective-permute-done.10, ...), kind=kLoop, calls=%fused_computation.62 | loop fusion | flops 540672 | bytes 786432 | tf_op jit(solution)/shard_map/convert_element_type | solution.py:263
  (53 shorter events, 3.0 us)
Async XLA Ops:
  0.0 108.1 %copy-start = (bf16[1536,2,256]{2,1,0:T(2,128)(2,1)S(1)}, bf16[1536,2,256]{2,1,0:T(2,128)(2,1)}, u32[]{:S(2)}) copy-start(bf16[1536,2,256]{2,1,0:T(2,128)(2,1)} %param.24) | copy-start | bytes 4718596
  0.9 15.8 %collective-permute-start.2 = (bf16[2,128,128]{2,1,0:T(8,128)(2,1)S(1)}, bf16[2,128,128]{2,1,0:T(8,128)(2,1)S(1)}, u32[]{:S(2)}, u32[]{:S(2)}) collective-permute-start(bf16[2,128,128]{2,1,0:T(8,128)(2,1)S(1)} %pad_maximum_fusion.2), channel_id=1, source_target_pairs={{0,4},{4,8},{8,12},{12,16},{16,20},{20,24},{24,28},{1,5},{5,9},{9,... | collective-permute-start | bytes 196616 | tf_op jit(solution)/shard_map/ppermute | solution.py:17
  3.3 13.4 %collective-permute-start.1 = (bf16[2,128,128]{2,1,0:T(8,128)(2,1)S(1)}, bf16[2,128,128]{2,1,0:T(8,128)(2,1)S(1)}, u32[]{:S(2)}, u32[]{:S(2)}) collective-permute-start(bf16[2,128,128]{2,1,0:T(8,128)(2,1)S(1)} %pad_maximum_fusion.2), channel_id=1, source_target_pairs={{0,8},{4,12},{8,16},{12,20},{16,24},{20,28},{1,9},{5,13},{9,17},{1... | collective-permute-start | bytes 196616 | tf_op jit(solution)/shard_map/ppermute | solution.py:17
  7.7 9.0 %collective-permute-start = (bf16[2,128,128]{2,1,0:T(8,128)(2,1)S(1)}, bf16[2,128,128]{2,1,0:T(8,128)(2,1)S(1)}, u32[]{:S(2)}, u32[]{:S(2)}) collective-permute-start(bf16[2,128,128]{2,1,0:T(8,128)(2,1)S(1)} %pad_maximum_fusion.2), channel_id=1, source_target_pairs={{0,12},{4,16},{8,20},{12,24},{16,28},{1,13},{5,17},{9,21},{13,25},... | collective-permute-start | bytes 196616 | tf_op jit(solution)/shard_map/ppermute | solution.py:17
  12.0 14.7 %collective-permute-start.3 = (bf16[384,768]{1,0:T(8,128)(2,1)}, bf16[384,768]{1,0:T(8,128)(2,1)S(1)}, u32[]{:S(2)}, u32[]{:S(2)}) collective-permute-start(bf16[384,768]{1,0:T(8,128)(2,1)} %param.18), channel_id=1, source_target_pairs={{0,16},{16,0},{1,17},{17,1},{2,18},{18,2},{3,19},{19,3},{4,20},{20... | collective-permute-start | bytes 1769480 | tf_op jit(solution)/shard_map/ppermute | solution.py:71
  17.9 1.1 copy-start.2
  18.4 20.0 %copy-start.3 = (bf16[32,1536]{1,0:T(8,128)(2,1)S(1)}, bf16[32,1536]{1,0:T(8,128)(2,1)}, u32[]{:S(2)}) copy-start(bf16[32,1536]{1,0:T(8,128)(2,1)} %param.16) | copy-start | bytes 294916
  19.3 19.4 %copy-start.6 = (f32[1536]{0:T(1024)S(1)}, f32[1536]{0:T(1024)}, u32[]{:S(2)}) copy-start(f32[1536]{0:T(1024)} %param.19) | copy-start | bytes 18436
  27.1 6.3 %collective-permute-start.6 = (bf16[32,1536]{1,0:T(8,128)(2,1)S(1)}, bf16[32,1536]{1,0:T(8,128)(2,1)S(1)}, u32[]{:S(2)}, u32[]{:S(2)}) collective-permute-start(bf16[32,1536]{1,0:T(8,128)(2,1)S(1)} %get-tuple-element.15), channel_id=1, source_target_pairs={{0,3},{1,0},{2,1},{3,2},{4,7},{5,4},{6,5},{7,6},{8,11},{9,8},{10,9... | collective-permute-start | bytes 294920 | tf_op jit(solution)/shard_map/ppermute | solution.py:67
  30.7 7.7 %collective-permute-start.5 = (bf16[32,1536]{1,0:T(8,128)(2,1)S(1)}, bf16[32,1536]{1,0:T(8,128)(2,1)S(1)}, u32[]{:S(2)}, u32[]{:S(2)}) collective-permute-start(bf16[32,1536]{1,0:T(8,128)(2,1)S(1)} %get-tuple-element.16), channel_id=1, source_target_pairs={{0,2},{1,3},{2,0},{3,1},{4,6},{5,7},{6,4},{7,5},{8,10},{9,11},{10,... | collective-permute-start | bytes 294920 | tf_op jit(solution)/shard_map/ppermute | solution.py:67
  30.7 7.7 %collective-permute-start.4 = (bf16[32,1536]{1,0:T(8,128)(2,1)S(1)}, bf16[32,1536]{1,0:T(8,128)(2,1)S(1)}, u32[]{:S(2)}, u32[]{:S(2)}) collective-permute-start(bf16[32,1536]{1,0:T(8,128)(2,1)S(1)} %get-tuple-element.14), channel_id=1, source_target_pairs={{0,1},{1,2},{2,3},{3,0},{4,5},{5,6},{6,7},{7,4},{8,9},{9,10},{10,1... | collective-permute-start | bytes 294920 | tf_op jit(solution)/shard_map/ppermute | solution.py:67
  40.5 38.7 %all-to-all-start = ((bf16[16,18,1536]{2,1,0:T(8,128)(2,1)}), bf16[16,18,1536]{2,1,0:T(8,128)(2,1)S(1)}, u32[]{:S(2)}, u32[]{:S(2)}) async-start(bf16[16,18,1536]{2,1,0:T(8,128)(2,1)} %reshape.190), calls=%async_computation | async-start | bytes 2359296 | tf_op jit(solution)/shard_map/all_to_all | solution.py:227
  45.2 37.6 %collective-permute-start.13 = (bf16[1,768,1024]{2,1,0:T(8,128)(2,1)}, bf16[1,768,1024]{2,1,0:T(8,128)(2,1)}, u32[]{:S(2)}, u32[]{:S(2)}) collective-permute-start(bf16[1,768,1024]{2,1,0:T(8,128)(2,1)} %param.22), channel_id=1, source_target_pairs={{0,16},{16,0},{1,17},{17,1},{2,18},{18,2},{3,19},{19,3},{4,20},{20... | collective-permute-start | bytes 4718600 | tf_op jit(solution)/shard_map/ppermute | solution.py:71
  47.0 52.1 %collective-permute-start.14 = (bf16[1,768,512]{2,1,0:T(8,128)(2,1)}, bf16[1,768,512]{2,1,0:T(8,128)(2,1)}, u32[]{:S(2)}, u32[]{:S(2)}) collective-permute-start(bf16[1,768,512]{2,1,0:T(8,128)(2,1)} %param.23), channel_id=1, source_target_pairs={{0,16},{16,0},{1,17},{17,1},{2,18},{18,2},{3,19},{19,3},{4,20},{20... | collective-permute-start | bytes 2359304 | tf_op jit(solution)/shard_map/ppermute | solution.py:71
  48.0 60.1 %collective-permute-start.9 = (bf16[32,1536]{1,0:T(8,128)(2,1)S(1)}, bf16[32,1536]{1,0:T(8,128)(2,1)S(1)}, u32[]{:S(2)}, u32[]{:S(2)}) collective-permute-start(bf16[32,1536]{1,0:T(8,128)(2,1)S(1)} %fusion.34), channel_id=1, source_target_pairs={{0,3},{1,0},{2,1},{3,2},{4,7},{5,4},{6,5},{7,6},{8,11},{9,8},{10,9... | collective-permute-start | bytes 294920 | tf_op jit(solution)/shard_map/ppermute | solution.py:67
  51.7 56.4 %collective-permute-start.8 = (bf16[32,1536]{1,0:T(8,128)(2,1)S(1)}, bf16[32,1536]{1,0:T(8,128)(2,1)S(1)}, u32[]{:S(2)}, u32[]{:S(2)}) collective-permute-start(bf16[32,1536]{1,0:T(8,128)(2,1)S(1)} %fusion.34), channel_id=1, source_target_pairs={{0,2},{1,3},{2,0},{3,1},{4,6},{5,7},{6,4},{7,5},{8,10},{9,11},{10,... | collective-permute-start | bytes 294920 | tf_op jit(solution)/shard_map/ppermute | solution.py:67
  51.7 56.4 %collective-permute-start.7 = (bf16[32,1536]{1,0:T(8,128)(2,1)S(1)}, bf16[32,1536]{1,0:T(8,128)(2,1)S(1)}, u32[]{:S(2)}, u32[]{:S(2)}) collective-permute-start(bf16[32,1536]{1,0:T(8,128)(2,1)S(1)} %fusion.34), channel_id=1, source_target_pairs={{0,1},{1,2},{2,3},{3,0},{4,5},{5,6},{6,7},{7,4},{8,9},{9,10},{10,1... | collective-permute-start | bytes 294920 | tf_op jit(solution)/shard_map/ppermute | solution.py:67
  85.0 1.1 copy-start.1
  101.8 5.9 %copy-start.4 = (bf16[1536,16]{0,1:T(8,128)(2,1)S(1)}, bf16[1536,16]{0,1:T(8,128)(2,1)}, u32[]{:S(2)}) copy-start(bf16[1536,16]{0,1:T(8,128)(2,1)} %param.20) | copy-start | bytes 147460
  101.8 6.1 %copy-start.5 = (s32[32,6]{0,1:T(8,128)S(1)}, s32[32,6]{0,1:T(8,128)}, u32[]{:S(2)}) copy-start(s32[32,6]{0,1:T(8,128)} %param.21) | copy-start | bytes 2308
  101.8 40.0 %all-to-all-start.1 = ((bf16[16,18,1536]{2,1,0:T(8,128)(2,1)}), bf16[16,18,1536]{2,1,0:T(8,128)(2,1)}, u32[]{:S(2)}, u32[]{:S(2)}) async-start(bf16[16,18,1536]{2,1,0:T(8,128)(2,1)} %maximum_bitcast_fusion), calls=%async_computation.1 | async-start | bytes 2359296 | tf_op jit(solution)/shard_map/all_to_all | solution.py:253
  108.1 1.1 copy-start.7
  110.2 36.1 %collective-permute-start.12 = (bf16[32,1536]{1,0:T(8,128)(2,1)}, bf16[32,1536]{1,0:T(8,128)(2,1)}, u32[]{:S(2)}, u32[]{:S(2)}) collective-permute-start(bf16[32,1536]{1,0:T(8,128)(2,1)} %get-tuple-element.12), channel_id=1, source_target_pairs={{0,1},{1,2},{2,3},{3,0},{4,5},{5,6},{6,7},{7,4},{8,9},{9,10},{10,1... | collective-permute-start | bytes 294920 | tf_op jit(solution)/shard_map/ppermute | solution.py:67
  112.1 34.2 %collective-permute-start.11 = (bf16[32,1536]{1,0:T(8,128)(2,1)}, bf16[32,1536]{1,0:T(8,128)(2,1)}, u32[]{:S(2)}, u32[]{:S(2)}) collective-permute-start(bf16[32,1536]{1,0:T(8,128)(2,1)} %get-tuple-element.13), channel_id=1, source_target_pairs={{0,2},{1,3},{2,0},{3,1},{4,6},{5,7},{6,4},{7,5},{8,10},{9,11},{10,... | collective-permute-start | bytes 294920 | tf_op jit(solution)/shard_map/ppermute | solution.py:67
  114.5 31.9 %collective-permute-start.10 = (bf16[32,1536]{1,0:T(8,128)(2,1)}, bf16[32,1536]{1,0:T(8,128)(2,1)}, u32[]{:S(2)}, u32[]{:S(2)}) collective-permute-start(bf16[32,1536]{1,0:T(8,128)(2,1)} %get-tuple-element.11), channel_id=1, source_target_pairs={{0,3},{1,0},{2,1},{3,2},{4,7},{5,4},{6,5},{7,6},{8,11},{9,8},{10,9... | collective-permute-start | bytes 294920 | tf_op jit(solution)/shard_map/ppermute | solution.py:67

commit v2 on v1

--- a/solution.py
+++ b/solution.py
@@ -3,6 +3,8 @@
 import jax
 import jax.numpy as jnp
 from jax import lax
+from jax.experimental import pallas as pl
+from jax.experimental.pallas import tpu as pltpu
 from jax.sharding import PartitionSpec as P
 
 HEAD = 128
@@ -107,6 +109,318 @@
         preferred_element_type=jnp.float32,
     )
     return acc / jnp.sum(weights, axis=-1, keepdims=True)
+
+
+MESH = pl.DeviceIdType.MESH
+LANES = 128
+LOW = 64
+
+
+def remote(src, dst, sends, recvs, at, device):
+    return pltpu.make_async_remote_copy(
+        src_ref=src,
+        dst_ref=dst,
+        send_sem=sends.at[at],
+        recv_sem=recvs.at[at],
+        device_id=device,
+        device_id_type=MESH,
+    )
+
+
+def front_kernel(
+    lengths, q, k, v, residual, w_own, gain, router, ids, gate_up, down,
+    stream, gathered, gate_full, down_full,
+    kv, w_other, att, partial, arrived,
+    kv_send, kv_recv, sum_send, sum_recv, tok_send, tok_recv, big_send, big_recv, local_sem,
+):
+    grp, ctx, exp = lax.axis_index("group"), lax.axis_index("ctx"), lax.axis_index("exp")
+    block = grp * 4 + ctx
+
+    def at_block(by):
+        other = (block + by) % 8
+        return (other // 4, other % 4, exp)
+
+    def at_exp(by):
+        return (grp, ctx, (exp + by) % 4)
+
+    y_peer = (grp, (ctx + 2) % 4, exp)
+    core_peer = (grp, ctx + 1 - 2 * (ctx % 2), exp)
+    x_peer = (1 - grp, ctx, exp)
+    barrier = pltpu.get_barrier_semaphore()
+    for by in range(1, 8):
+        pl.semaphore_signal(barrier, inc=1, device_id=at_block(by), device_id_type=MESH)
+    for by in range(1, 4):
+        pl.semaphore_signal(barrier, inc=1, device_id=at_exp(by), device_id_type=MESH)
+    pl.semaphore_wait(barrier, 10)
+
+    kv_copies = []
+    for by in (1, 2, 3):
+        for which, ref in ((0, k), (1, v)):
+            copy = remote(
+                ref, kv.at[by - 1, which], kv_send, kv_recv, 2 * (by - 1) + which, at_block(by)
+            )
+            copy.start()
+            kv_copies.append(copy)
+    w_copy = remote(w_own, w_other, big_send, big_recv, 0, x_peer)
+    w_copy.start()
+    half = gate_up.shape[1]
+    mine = pl.ds(pl.multiple_of(grp * half, half), half)
+    gate_local = pltpu.make_async_copy(gate_up, gate_full.at[:, mine], local_sem.at[0])
+    down_local = pltpu.make_async_copy(down, down_full.at[:, mine], local_sem.at[1])
+    gate_local.start()
+    down_local.start()
+
+    rows = q.shape[0]
+    pos = block * rows + lax.broadcasted_iota(jnp.int32, (rows, 1), 0)
+    start = jnp.zeros((rows, 1), jnp.int32)
+    end = 0
+    for doc in range(lengths.shape[0]):
+        end = end + lengths[doc]
+        start = start + jnp.where(pos >= end, lengths[doc], 0)
+    key_pos = (block - 3) * rows + lax.broadcasted_iota(jnp.int32, (rows, 4 * rows), 1)
+    allowed = (key_pos <= pos) & (key_pos >= start)
+    for copy in kv_copies:
+        copy.wait()
+    keys = [kv[2, 0], kv[1, 0], kv[0, 0], k[...]]
+    vals = jnp.concatenate([kv[2, 1], kv[1, 1], kv[0, 1], v[...]], axis=0)
+    keys = jnp.concatenate(keys, axis=0)
+    for head in range(q.shape[1] // HEAD):
+        cols = pl.ds(head * HEAD, HEAD)
+        scores = lax.dot_general(
+            q[:, cols], keys, (((1,), (1,)), ((), ())), preferred_element_type=jnp.float32
+        ) * (1.0 / math.sqrt(HEAD))
+        scores = jnp.where(allowed, scores, neg_big)
+        top = jnp.max(scores, axis=-1, keepdims=True)
+        weights = jnp.where(allowed, jnp.exp(scores - top), 0.0)
+        total = jnp.sum(weights, axis=-1, keepdims=True)
+        acc = jnp.dot(
+            weights.astype(jnp.bfloat16), vals, preferred_element_type=jnp.float32
+        )
+        att[:, cols] = (acc / total).astype(jnp.bfloat16)
+
+    w_copy.wait()
+    theirs = gate_full.at[:, mine]
+    gate_copy = remote(gate_up, theirs, big_send, big_recv, 1, x_peer)
+    down_copy = remote(down, down_full.at[:, mine], big_send, big_recv, 2, x_peer)
+    gate_copy.start()
+    down_copy.start()
+
+    wide = w_own.shape[1]
+    own_cols = pl.ds(pl.multiple_of(grp * wide, wide), wide)
+    other_cols = pl.ds(pl.multiple_of((1 - grp) * wide, wide), wide)
+    tok = residual.shape[0]
+    sums = []
+    for by in (2, 1, 3, 0):
+        piece = att[pl.ds(pl.multiple_of(((exp + by) % 4) * tok, tok), tok), :]
+        partial[by, :, own_cols] = jnp.dot(
+            piece, w_own[...], preferred_element_type=jnp.float32
+        ).astype(jnp.bfloat16)
+        partial[by, :, other_cols] = jnp.dot(
+            piece, w_other[...], preferred_element_type=jnp.float32
+        ).astype(jnp.bfloat16)
+        if by:
+            copy = remote(
+                partial.at[by], arrived.at[by - 1], sum_send, sum_recv, by - 1, at_exp(by)
+            )
+            copy.start()
+            sums.append(copy)
+    total = partial[0].astype(jnp.float32)
+    for copy in sums:
+        copy.wait()
+    for by in range(3):
+        total = total + arrived[by].astype(jnp.float32)
+    held = (residual[...].astype(jnp.float32) + total).astype(jnp.bfloat16)
+    stream[...] = held
+    wide_f = held.astype(jnp.float32)
+    normed = (
+        wide_f
+        * lax.rsqrt(jnp.mean(wide_f * wide_f, axis=-1, keepdims=True) + 1e-05)
+        * gain[...]
+    ).astype(jnp.bfloat16)
+    width = normed.shape[1]
+    logits = jnp.dot(normed, router[...], preferred_element_type=jnp.float32)
+    lane = lax.broadcasted_iota(jnp.int32, (tok, LANES), 1)
+    expert = jnp.where(lane >= LOW, lane - LOW, lane)
+    named = jnp.zeros((tok, LANES), jnp.float32)
+    for route in range(ids.shape[1]):
+        named = named + jnp.where(ids[:, route : route + 1] == expert, 1.0, 0.0)
+    raw = jnp.where(named > 0.0, 1.0 / (1.0 + jnp.exp(-logits)), 0.0)
+    sum_raw = jnp.sum(jnp.where(lane < LOW, raw, 0.0), axis=-1, keepdims=True)
+    gates = raw / sum_raw
+    high = gates.astype(jnp.bfloat16)
+    rest = (gates - high.astype(jnp.float32)).astype(jnp.bfloat16)
+    gathered[0, :, :width] = normed
+    gathered[0, :, width:] = jnp.where(
+        lane < LOW, high.astype(jnp.float32), rest.astype(jnp.float32)
+    ).astype(jnp.bfloat16)
+
+    def passing(source, target, device):
+        copy = remote(gathered.at[source], gathered.at[target], tok_send, tok_recv, target, device)
+        copy.start()
+        return copy
+
+    first = {by: passing(0, by, at_exp(by)) for by in (2, 1, 3)}
+    second, third = {}, []
+    for by in (0, 1, 2, 3):
+        if by:
+            first[by].wait_recv()
+        second[by] = passing(by, 8 + by, y_peer)
+        third.append(passing(by, 4 + by, core_peer))
+    for by in (0, 1, 2, 3):
+        second[by].wait_recv()
+        third.append(passing(8 + by, 12 + by, core_peer))
+    for copy in third:
+        copy.wait_recv()
+    for copy in [*first.values(), *second.values(), *third]:
+        copy.wait_send()
+    gate_local.wait()
+    down_local.wait()
+    gate_copy.wait()
+    down_copy.wait()
+
+
+def back_kernel(
+    parts, shared, stream, out,
+    one_in, one_sum, two_in, two_sum, three_in,
+    one_send, one_recv, two_send, two_recv, three_send, three_recv,
+):
+    grp, ctx, exp = lax.axis_index("group"), lax.axis_index("ctx"), lax.axis_index("exp")
+    y_peer = (grp, (ctx + 2) % 4, exp)
+    core_peer = (grp, ctx + 1 - 2 * (ctx % 2), exp)
+
+    def at_exp(by):
+        return (grp, ctx, (exp + by) % 4)
+
+    barrier = pltpu.get_barrier_semaphore()
+    for peer in (y_peer, core_peer, at_exp(1), at_exp(2), at_exp(3)):
+        pl.semaphore_signal(barrier, inc=1, device_id=peer, device_id_type=MESH)
+    pl.semaphore_wait(barrier, 5)
+
+    order = (2, 1, 3, 0)
+    one = {}
+    for far in (1, 0):
+        for by in order:
+            at = 4 * far + by
+            one[at] = remote(
+                parts.at[8 * far + 4 + by], one_in.at[at], one_send, one_recv, at, core_peer
+            )
+            one[at].start()
+    two = {}
+    for by in order:
+        one[4 + by].wait_recv()
+        one_sum[by] = (
+            parts[8 + by].astype(jnp.float32) + one_in[4 + by].astype(jnp.float32)
+        ).astype(jnp.bfloat16)
+        two[by] = remote(one_sum.at[by], two_in.at[by], two_send, two_recv, by, y_peer)
+        two[by].start()
+    three = []
+    for by in order:
+        one[by].wait_recv()
+        near = (
+            parts[by].astype(jnp.float32)
+            + one_in[by].astype(jnp.float32)
+            + shared[by].astype(jnp.float32)
+        )
+        two[by].wait_recv()
+        near = near + two_in[by].astype(jnp.float32)
+        if by:
+            two_sum[by - 1] = near.astype(jnp.bfloat16)
+            copy = remote(
+                two_sum.at[by - 1], three_in.at[by - 1], three_send, three_recv, by - 1,
+                at_exp(4 - by),
+            )
+            copy.start()
+            three.append(copy)
+        else:
+            total = near + stream[...].astype(jnp.float32)
+    for copy in three:
+        copy.wait_recv()
+    for by in range(3):
+        total = total + three_in[by].astype(jnp.float32)
+    out[...] = total.astype(jnp.bfloat16)
+    for copy in [*one.values(), *two.values(), *three]:
+        copy.wait_send()
+
+
+def with_kernels(
+    queries, keys, values, residual_in, doc_lengths, w_out, norm_gain, router, expert_ids,
+    expert_gate_up, expert_down, shared_gate_up, shared_down,
+):
+    bf = jnp.bfloat16
+    tok, width = residual_in.shape
+    experts = router.shape[1]
+    heads_dev = queries.shape[1]
+    rows = queries.shape[0]
+    pad = jnp.pad(router, ((0, 0), (0, LOW - experts)))
+    vmem, hbm = pl.BlockSpec(memory_space=pltpu.VMEM), pl.BlockSpec(memory_space=pl.ANY)
+    smem = pl.BlockSpec(memory_space=pltpu.SMEM)
+    dma = pltpu.SemaphoreType.DMA
+    up_shape, down_shape = expert_gate_up.shape, expert_down.shape
+    stream, gathered, gate_full, down_full = pl.pallas_call(
+        front_kernel,
+        out_shape=(
+            jax.ShapeDtypeStruct((tok, width), bf),
+            jax.ShapeDtypeStruct((16, tok, width + LANES), bf),
+            jax.ShapeDtypeStruct((up_shape[0], 2 * up_shape[1], up_shape[2]), bf),
+            jax.ShapeDtypeStruct((down_shape[0], 2 * down_shape[1], down_shape[2]), bf),
+        ),
+        in_specs=[smem, *[vmem] * 8, hbm, hbm],
+        out_specs=(vmem, vmem, hbm, hbm),
+        scratch_shapes=[
+            pltpu.VMEM((3, 2, rows, HEAD), bf),
+            pltpu.VMEM(w_out.shape, bf),
+            pltpu.VMEM((rows, heads_dev), bf),
+            pltpu.VMEM((4, tok, width), bf),
+            pltpu.VMEM((3, tok, width), bf),
+            dma((6,)), dma((6,)), dma((3,)), dma((3,)), dma((16,)), dma((16,)),
+            dma((3,)), dma((3,)), dma((2,)),
+        ],
+        compiler_params=pltpu.CompilerParams(
+            collective_id=0, has_side_effects=True, vmem_limit_bytes=24 * 2**20
+        ),
+    )(
+        doc_lengths, queries, keys, values, residual_in, w_out, norm_gain.reshape(1, -1),
+        jnp.concatenate([pad, pad], axis=1), expert_ids, expert_gate_up, expert_down,
+    )
+    tokens = gathered[:, :, :width].reshape(16 * tok, width)
+    coded = gathered[:, :, width:].reshape(16 * tok, LANES).astype(jnp.float32)
+    gates = coded[:, :LOW] + coded[:, LOW:]
+    local = up_shape[0]
+    first = (lax.axis_index("ctx") * lax.axis_size("exp") + lax.axis_index("exp")) * local
+    hidden = down_shape[2]
+    total = jnp.zeros((16 * tok, width), jnp.float32)
+    for e in range(local):
+        pre = jnp.dot(tokens, gate_full[e], preferred_element_type=jnp.float32)
+        act = (jax.nn.silu(pre[:, :hidden]) * pre[:, hidden:]).astype(bf)
+        made = lax.dot_general(
+            act, down_full[e], (((1,), (1,)), ((), ())), preferred_element_type=jnp.float32
+        ).astype(bf)
+        is_mine = jnp.arange(LOW, dtype=jnp.int32)[None, :] == first + e
+        gate = jnp.sum(jnp.where(is_mine, gates, 0.0), axis=1, keepdims=True)
+        total = total + gate * made.astype(jnp.float32)
+    near = tokens[: 4 * tok]
+    shared_pre = jnp.einsum(
+        "td,dkf->tkf", near, shared_gate_up, preferred_element_type=jnp.float32
+    )
+    shared_act = (jax.nn.silu(shared_pre[:, 0]) * shared_pre[:, 1]).astype(bf)
+    shared = matmul(shared_act, shared_down).reshape(4, tok, width)
+    return pl.pallas_call(
+        back_kernel,
+        out_shape=jax.ShapeDtypeStruct((tok, width), bf),
+        in_specs=[vmem] * 3,
+        out_specs=vmem,
+        scratch_shapes=[
+            pltpu.VMEM((8, tok, width), bf),
+            pltpu.VMEM((4, tok, width), bf),
+            pltpu.VMEM((4, tok, width), bf),
+            pltpu.VMEM((3, tok, width), bf),
+            pltpu.VMEM((3, tok, width), bf),
+            dma((8,)), dma((8,)), dma((4,)), dma((4,)), dma((3,)), dma((3,)),
+        ],
+        compiler_params=pltpu.CompilerParams(
+            collective_id=1, has_side_effects=True, vmem_limit_bytes=24 * 2**20
+        ),
+    )(total.astype(bf).reshape(16, tok, width), shared, stream)
 
 
 def on_device(
@@ -280,6 +594,8 @@
         P("exp", None),
     )
     out_specs = P(("group", "ctx", "exp"), None)
+    sizes = (mesh.shape["group"], mesh.shape["ctx"], mesh.shape["exp"])
+    body = with_kernels if sizes == (2, 4, 4) else on_device
     return jax.shard_map(
-        on_device, mesh=mesh, in_specs=in_specs, out_specs=out_specs, check_vma=False
-    )
+        body, mesh=mesh, in_specs=in_specs, out_specs=out_specs, check_vma=False
+    )

time: 149 us -> 105 us (0.70)
  Pallas kernels: 0 us -> 92.4 us
  waiting for transfers between devices: 80.2 us -> 0 us
  starting transfers between devices: 39 us -> 0 us
  other arithmetic: 10.2 us -> 0.48 us
  matrix products: 8.89 us -> 3.57 us
    pallas_call x0 -> x2, Pallas kernels: none -> 92.4 us  [the longest x1 73.1 us: with_kernels(): pl.pallas_call(front_kernel, out_shape=(jax.ShapeDtypeStruct((tok, width)...]
    all_to_all x2 -> x0, waiting for transfers between devices: 52.3 us -> none  [the longest x1 26.4 us: on_device(): lax.all_to_all(outgoing, ('ctx', 'exp'), split_axis=0, concat_axis=0, til...]
    ppermute x15 -> x0, starting transfers between devices: 28.4 us -> none  [the longest x9 15.2 us: turned(): lax.ppermute(shard, axis, [(i, (i + by) % length) for i in range(length)])]
    ppermute x15 -> x0, waiting for transfers between devices: 27.9 us -> none  [the longest x3 21.3 us: swapped(): return lax.ppermute(shard, 'group', [(0, 1), (1, 0)])]
    all_to_all x2 -> x0, starting transfers between devices: 10.6 us -> none  [the longest x1 5.92 us: on_device(): lax.all_to_all(result.reshape(arrived.shape), ('ctx', 'exp'), split_axis=...]
    dot_general x9 -> x3, matrix products: 8.03 us -> 3.29 us  [the longest x1 1.85 us: with_kernels(): pre = jnp.dot(tokens, gate_full[e], preferred_element_type=jnp.float32)]
    reduce_sum x9 -> x1, other arithmetic: 3.8 us -> 0.23 us  [with_kernels(): gate = jnp.sum(jnp.where(is_mine, gates, 0.0), axis=1, keepdims=True)]
    unnamed x18 -> x23, local copies, waits for them, and re-layouts: 3.81 us -> 6.13 us
  transfers between devices with their start and end apart: 17 -> 0, of which waited for: 7 -> 0; matrix products, arithmetic and copies ran while one was open for 15% -> 0% of each run, Pallas kernels for 0% -> 0%
where the time goes in v2:
time: 105 us
  Pallas kernels  92.4 us (88%)
  local copies, waits for them, and re-layouts  8.27 us (8%)
  matrix products  3.57 us (3%)
    pallas_call x1, Pallas kernels, with_kernels(): pl.pallas_call(front_kernel, out_shape=(jax.ShapeDtypeStruct((tok, width)...  73.1 us
    pallas_call x1, Pallas kernels, with_kernels(): pl.pallas_call(back_kernel, out_shape=jax.ShapeDtypeStruct((tok, width),...  19.3 us
    unnamed x23, local copies, waits for them, and re-layouts  6.13 us

profile of v2, /device:TPU:0, one launch (start us, length us, event | category | flops | bytes accessed | tf_op | source)
XLA Modules:
  0.0 105.0 jit_solution(13287667077364963362)
XLA Ops:
  0.0 0.0 copy-start
  0.0 0.0 copy-start.1
  0.0 0.0 copy-start.8
  0.0 0.0 copy-start.5
  0.0 0.0 copy-start.7
  0.0 0.0 copy-start.6
  0.0 0.0 copy-start.4
  0.1 0.9 reshape.22.gain
  0.9 0.8 copy.15.ids
  1.7 1.7 %copy.14 = bf16[1536,16]{1,0:T(8,128)(2,1)} copy(bf16[1536,16]{0,1:T(8,128)(2,1)} %param.20) | data formatting | bytes 98304 | tf_op args[7]
  3.5 1.1 %pad.4 = bf16[1536,64]{1,0:T(8,128)(2,1)S(1)} pad(bf16[1536,16]{1,0:T(8,128)(2,1)} %copy.14, bf16[]{:T(256)} %constant.16.clone.1), padding=0_0x0_48 | pad | bytes 245762 | tf_op jit(solution)/shard_map/jit(_pad)/pad | solution.py:354
  4.5 0.2 pad_maximum_fusion.router
  4.8 0.0 copy-done.1
  4.8 0.0 copy-done.8
  4.8 0.0 copy-done.5
  4.8 0.0 copy-done.7
  4.8 0.0 copy-done.6
  4.8 0.0 copy-done.4
  4.8 0.0 copy-start.2
  4.8 1.1 %copy-done.2 = bf16[1,768,512]{2,1,0:T(8,128)(2,1)S(1)} copy-done((bf16[1,768,512]{2,1,0:T(8,128)(2,1)S(1)}, bf16[1,768,512]{2,1,0:T(8,128)(2,1)}, u32[]{:S(2)}) %copy-start.2) | copy-done | bytes 786456
  6.0 0.0 copy-start.3
  6.0 1.1 %copy-done.3 = bf16[384,768]{1,0:T(8,128)(2,1)S(1)} copy-done((bf16[384,768]{1,0:T(8,128)(2,1)S(1)}, bf16[384,768]{1,0:T(8,128)(2,1)}, u32[]{:S(2)}) %copy-start.3) | copy-done | bytes 589848
  7.0 73.1 %shard_map.127 = (bf16[32,1536]{1,0:T(8,128)(2,1)S(1)}, bf16[16,32,1664]{2,1,0:T(8,128)(2,1)S(1)}, bf16[1,1536,1024]{2,1,0:T(8,128)(2,1)S(1)}, bf16[1,1536,512]{2,1,0:T(8,128)(2,1)S(1)}) custom-call(s32[4]{0:T(128)S(1)} %copy-done.8, bf16[128,384]{1,0:T(8,128)(2,1)S(1)} %copy-done.4, bf16[128,128]{1,0:T(8,128)(2,1)S(1)} %copy-done.6, ...), custom_call_target="tpu_custom_call" | custom-call | tf_op jit(solution)/shard_map/pallas_call | solution.py:359
  80.2 0.2 fusion.9
  80.5 0.2 slice.34
  80.6 1.9 %fusion = f32[512,1024]{1,0:T(8,128)S(1)} fusion(bf16[512,1536]{1,0:T(8,128)(2,1)S(1)} %bitcast.31, bf16[1,1536,1024]{2,1,0:T(8,128)(2,1)S(1)} %get-tuple-element.10), kind=kOutput, calls=%fused_computation | convolution fusion | flops 1610612736 | bytes 6815744 | tf_op jit(solution)/shard_map/dot_general | solution.py:393
  82.5 1.1 %multiply_convert_fusion = bf16[512,1536]{1,0:T(8,128)(2,1)S(1)} fusion(bf16[1,1536,512]{2,1,0:T(8,128)(2,1)S(1)} %get-tuple-element.11, f32[512]{0:T(512)S(1)} %fusion.9, f32[512,1024]{1,0:T(8,128)S(1)} %fusion), kind=kOutput, calls=%fused_computation.2 | convolution fusion | flops 810024960 | bytes 5244928 | tf_op jit(solution)/shard_map/dot_general | solution.py:395
  83.6 0.0 copy-start.9
  83.6 0.0 copy-done
  83.6 0.4 fusion.3
  84.0 0.7 copy-done.9
  84.7 0.3 convolution_convert_fusion.1
  85.0 19.3 %shard_map.128 = bf16[32,1536]{1,0:T(8,128)(2,1)S(1)} custom-call(bf16[16,32,1536]{2,1,0:T(8,128)(2,1)S(1)} %bitcast.29, bf16[4,32,1536]{2,1,0:T(8,128)(2,1)S(1)} %bitcast.30, bf16[32,1536]{1,0:T(8,128)(2,1)S(1)} %get-tuple-element.12.stream), custom_call_target="tpu_custom_call" | custom-call | tf_op jit(solution)/shard_map/pallas_call | solution.py:407
  104.3 0.6 copy.20
  (4 shorter events, 0.1 us)
Async XLA Ops:
  0.0 83.6 %copy-start = (bf16[1536,2,256]{2,1,0:T(2,128)(2,1)S(1)}, bf16[1536,2,256]{2,1,0:T(2,128)(2,1)}, u32[]{:S(2)}) copy-start(bf16[1536,2,256]{2,1,0:T(2,128)(2,1)} %param.24) | copy-start | bytes 4718596
  0.0 4.8 %copy-start.1 = (bf16[1,768,1024]{2,1,0:T(8,128)(2,1)S(1)}, bf16[1,768,1024]{2,1,0:T(8,128)(2,1)}, u32[]{:S(2)}) copy-start(bf16[1,768,1024]{2,1,0:T(8,128)(2,1)} %gate_up.1) | copy-start | bytes 4718596
  0.0 4.8 %copy-start.8 = (s32[4]{0:T(128)S(1)}, s32[4]{0:T(128)}, u32[]{:S(2)}) copy-start(s32[4]{0:T(128)} %lengths.1) | copy-start | bytes 52
  0.0 4.8 %copy-start.5 = (bf16[32,1536]{1,0:T(8,128)(2,1)S(1)}, bf16[32,1536]{1,0:T(8,128)(2,1)}, u32[]{:S(2)}) copy-start(bf16[32,1536]{1,0:T(8,128)(2,1)} %residual.1) | copy-start | bytes 294916
  0.0 4.8 %copy-start.7 = (bf16[128,128]{1,0:T(8,128)(2,1)S(1)}, bf16[128,128]{1,0:T(8,128)(2,1)}, u32[]{:S(2)}) copy-start(bf16[128,128]{1,0:T(8,128)(2,1)} %v.1) | copy-start | bytes 98308
  0.0 4.8 %copy-start.6 = (bf16[128,128]{1,0:T(8,128)(2,1)S(1)}, bf16[128,128]{1,0:T(8,128)(2,1)}, u32[]{:S(2)}) copy-start(bf16[128,128]{1,0:T(8,128)(2,1)} %k.1) | copy-start | bytes 98308
  0.0 4.8 %copy-start.4 = (bf16[128,384]{1,0:T(8,128)(2,1)S(1)}, bf16[128,384]{1,0:T(8,128)(2,1)}, u32[]{:S(2)}) copy-start(bf16[128,384]{1,0:T(8,128)(2,1)} %q.1) | copy-start | bytes 294916
  4.8 1.1 %copy-start.2 = (bf16[1,768,512]{2,1,0:T(8,128)(2,1)S(1)}, bf16[1,768,512]{2,1,0:T(8,128)(2,1)}, u32[]{:S(2)}) copy-start(bf16[1,768,512]{2,1,0:T(8,128)(2,1)} %down.1) | copy-start | bytes 2359300
  6.0 1.1 %copy-start.3 = (bf16[384,768]{1,0:T(8,128)(2,1)S(1)}, bf16[384,768]{1,0:T(8,128)(2,1)}, u32[]{:S(2)}) copy-start(bf16[384,768]{1,0:T(8,128)(2,1)} %w_own.1) | copy-start | bytes 1769476
  83.6 1.1 %copy-start.9 = (bf16[256,1536]{1,0:T(8,128)(2,1)S(1)}, bf16[256,1536]{1,0:T(8,128)(2,1)}, u32[]{:S(2)}) copy-start(bf16[256,1536]{1,0:T(8,128)(2,1)} %param.25) | copy-start | bytes 2359300

commit v3 on v2

--- a/solution.py
+++ b/solution.py
@@ -130,8 +130,9 @@
 def front_kernel(
     lengths, q, k, v, residual, w_own, gain, router, ids, gate_up, down,
     stream, gathered, gate_full, down_full,
-    kv, w_other, att, partial, arrived,
-    kv_send, kv_recv, sum_send, sum_recv, tok_send, tok_recv, big_send, big_recv, local_sem,
+    kv, att, att_other, partial, arrived, crossing, crossed, table,
+    kv_send, kv_recv, sum_send, sum_recv, tok_send, tok_recv, big_send, big_recv, cross_send, cross_recv,
+    local_sem,
 ):
     grp, ctx, exp = lax.axis_index("group"), lax.axis_index("ctx"), lax.axis_index("exp")
     block = grp * 4 + ctx
@@ -161,9 +162,25 @@
             )
             copy.start()
             kv_copies.append(copy)
-    w_copy = remote(w_own, w_other, big_send, big_recv, 0, x_peer)
-    w_copy.start()
     half = gate_up.shape[1]
+    piece_rows = half // 6
+    bulk = []
+
+    def bulk_send(count):
+        for _ in range(count):
+            at = len(bulk)
+            src, full = (gate_up, gate_full) if at < 6 else (down, down_full)
+            from_row = (at % 6) * piece_rows
+            to_row = pl.multiple_of(grp * half + from_row, piece_rows)
+            copy = remote(
+                src.at[:, pl.ds(from_row, piece_rows)],
+                full.at[:, pl.ds(to_row, piece_rows)],
+                big_send, big_recv, at, x_peer,
+            )
+            copy.start()
+            bulk.append(copy)
+
+    bulk_send(3)
     mine = pl.ds(pl.multiple_of(grp * half, half), half)
     gate_local = pltpu.make_async_copy(gate_up, gate_full.at[:, mine], local_sem.at[0])
     down_local = pltpu.make_async_copy(down, down_full.at[:, mine], local_sem.at[1])
@@ -198,12 +215,14 @@
         )
         att[:, cols] = (acc / total).astype(jnp.bfloat16)
 
-    w_copy.wait()
-    theirs = gate_full.at[:, mine]
-    gate_copy = remote(gate_up, theirs, big_send, big_recv, 1, x_peer)
-    down_copy = remote(down, down_full.at[:, mine], big_send, big_recv, 2, x_peer)
-    gate_copy.start()
-    down_copy.start()
+    att_copy = remote(att, att_other, cross_send, cross_recv, 0, x_peer)
+    att_copy.start()
+    table[...] = jnp.zeros_like(table)
+    experts = router.shape[0]
+    table[:experts] = router[...]
+    table[LOW : LOW + experts] = router[...]
+    att_copy.wait()
+    bulk_send(1)
 
     wide = w_own.shape[1]
     own_cols = pl.ds(pl.multiple_of(grp * wide, wide), wide)
@@ -211,12 +230,10 @@
     tok = residual.shape[0]
     sums = []
     for by in (2, 1, 3, 0):
-        piece = att[pl.ds(pl.multiple_of(((exp + by) % 4) * tok, tok), tok), :]
-        partial[by, :, own_cols] = jnp.dot(
+        rows_at = pl.ds(pl.multiple_of(((exp + by) % 4) * tok, tok), tok)
+        piece = jnp.concatenate([att[rows_at, :], att_other[rows_at, :]], axis=0)
+        partial[by] = jnp.dot(
             piece, w_own[...], preferred_element_type=jnp.float32
-        ).astype(jnp.bfloat16)
-        partial[by, :, other_cols] = jnp.dot(
-            piece, w_other[...], preferred_element_type=jnp.float32
         ).astype(jnp.bfloat16)
         if by:
             copy = remote(
@@ -229,21 +246,40 @@
         copy.wait()
     for by in range(3):
         total = total + arrived[by].astype(jnp.float32)
-    held = (residual[...].astype(jnp.float32) + total).astype(jnp.bfloat16)
-    stream[...] = held
-    wide_f = held.astype(jnp.float32)
+    crossing[...] = total[tok:].astype(jnp.bfloat16)
+    cross_copy = remote(crossing, crossed, cross_send, cross_recv, 1, x_peer)
+    cross_copy.start()
+    stream[:, own_cols] = (
+        residual[:, own_cols].astype(jnp.float32) + total[:tok]
+    ).astype(jnp.bfloat16)
+    cross_copy.wait()
+    bulk_send(8)
+    stream[:, other_cols] = (
+        residual[:, other_cols].astype(jnp.float32) + crossed[...].astype(jnp.float32)
+    ).astype(jnp.bfloat16)
+    wide_f = stream[...].astype(jnp.float32)
     normed = (
         wide_f
         * lax.rsqrt(jnp.mean(wide_f * wide_f, axis=-1, keepdims=True) + 1e-05)
-        * gain[...]
+        * gain[...].reshape(1, -1)
     ).astype(jnp.bfloat16)
     width = normed.shape[1]
-    logits = jnp.dot(normed, router[...], preferred_element_type=jnp.float32)
+    logits = lax.dot_general(
+        normed, table[...], (((1,), (1,)), ((), ())), preferred_element_type=jnp.float32
+    )
     lane = lax.broadcasted_iota(jnp.int32, (tok, LANES), 1)
-    expert = jnp.where(lane >= LOW, lane - LOW, lane)
-    named = jnp.zeros((tok, LANES), jnp.float32)
-    for route in range(ids.shape[1]):
-        named = named + jnp.where(ids[:, route : route + 1] == expert, 1.0, 0.0)
+    row = lax.broadcasted_iota(jnp.int32, (LANES, tok), 0)
+    expert = jnp.where(row >= LOW, row - LOW, row)
+    columns = jnp.zeros((LANES, tok), jnp.float32)
+    for route in range(ids.shape[0]):
+        columns = columns + jnp.where(ids[route : route + 1, :] == expert, 1.0, 0.0)
+    across = lax.broadcasted_iota(jnp.int32, (tok, tok), 0)
+    along = lax.broadcasted_iota(jnp.int32, (tok, tok), 1)
+    eye = jnp.where(across == along, 1.0, 0.0).astype(jnp.bfloat16)
+    named = lax.dot_general(
+        eye, columns.astype(jnp.bfloat16), (((1,), (1,)), ((), ())),
+        preferred_element_type=jnp.float32,
+    )
     raw = jnp.where(named > 0.0, 1.0 / (1.0 + jnp.exp(-logits)), 0.0)
     sum_raw = jnp.sum(jnp.where(lane < LOW, raw, 0.0), axis=-1, keepdims=True)
     gates = raw / sum_raw
@@ -275,8 +311,8 @@
         copy.wait_send()
     gate_local.wait()
     down_local.wait()
-    gate_copy.wait()
-    down_copy.wait()
+    for copy in bulk:
+        copy.wait()
 
 
 def back_kernel(
@@ -348,10 +384,8 @@
 ):
     bf = jnp.bfloat16
     tok, width = residual_in.shape
-    experts = router.shape[1]
     heads_dev = queries.shape[1]
     rows = queries.shape[0]
-    pad = jnp.pad(router, ((0, 0), (0, LOW - experts)))
     vmem, hbm = pl.BlockSpec(memory_space=pltpu.VMEM), pl.BlockSpec(memory_space=pl.ANY)
     smem = pl.BlockSpec(memory_space=pltpu.SMEM)
     dma = pltpu.SemaphoreType.DMA
@@ -368,19 +402,22 @@
         out_specs=(vmem, vmem, hbm, hbm),
         scratch_shapes=[
             pltpu.VMEM((3, 2, rows, HEAD), bf),
-            pltpu.VMEM(w_out.shape, bf),
             pltpu.VMEM((rows, heads_dev), bf),
-            pltpu.VMEM((4, tok, width), bf),
-            pltpu.VMEM((3, tok, width), bf),
+            pltpu.VMEM((rows, heads_dev), bf),
+            pltpu.VMEM((4, 2 * tok, width // 2), bf),
+            pltpu.VMEM((3, 2 * tok, width // 2), bf),
+            pltpu.VMEM((tok, width // 2), bf),
+            pltpu.VMEM((tok, width // 2), bf),
+            pltpu.VMEM((LANES, width), bf),
             dma((6,)), dma((6,)), dma((3,)), dma((3,)), dma((16,)), dma((16,)),
-            dma((3,)), dma((3,)), dma((2,)),
+            dma((12,)), dma((12,)), dma((2,)), dma((2,)), dma((2,)),
         ],
         compiler_params=pltpu.CompilerParams(
             collective_id=0, has_side_effects=True, vmem_limit_bytes=24 * 2**20
         ),
     )(
-        doc_lengths, queries, keys, values, residual_in, w_out, norm_gain.reshape(1, -1),
-        jnp.concatenate([pad, pad], axis=1), expert_ids, expert_gate_up, expert_down,
+        doc_lengths, queries, keys, values, residual_in, w_out, norm_gain,
+        router.T, expert_ids.T, expert_gate_up, expert_down,
     )
     tokens = gathered[:, :, :width].reshape(16 * tok, width)
     coded = gathered[:, :, width:].reshape(16 * tok, LANES).astype(jnp.float32)

time: 105 us -> 104 us (level)
  Pallas kernels: 92.4 us -> 88.4 us
  local copies, waits for them, and re-layouts: 8.27 us -> 11.4 us
    unnamed x23 -> x27, local copies, waits for them, and re-layouts: 6.13 us -> 11.2 us
    pallas_call x1, Pallas kernels: 73.1 us -> 68.5 us  [with_kernels(): pl.pallas_call(front_kernel, out_shape=(jax.ShapeDtypeStruct((tok, width)...]
    pad x1 -> x0, local copies, waits for them, and re-layouts: 1.07 us -> none  [with_kernels(): pad = jnp.pad(router, ((0, 0), (0, LOW - experts)))]
where the time goes in v3:
time: 104 us
  Pallas kernels  88.4 us (85%)
  local copies, waits for them, and re-layouts  11.4 us (11%)
  matrix products  3.54 us (3%)
    pallas_call x1, Pallas kernels, with_kernels(): pl.pallas_call(front_kernel, out_shape=(jax.ShapeDtypeStruct((tok, width)...  68.5 us
    pallas_call x1, Pallas kernels, with_kernels(): pl.pallas_call(back_kernel, out_shape=jax.ShapeDtypeStruct((tok, width),...  19.8 us
    unnamed x27, local copies, waits for them, and re-layouts  11.2 us

profile of v3, /device:TPU:0, one launch (start us, length us, event | category | flops | bytes accessed | tf_op | source)
XLA Modules:
  0.0 103.7 jit_solution(3420747184503244532)
XLA Ops:
  0.0 0.0 copy-start
  0.0 0.0 copy-start.1
  0.0 1.5 %copy-done.1 = bf16[1,768,1024]{2,1,0:T(8,128)(2,1)S(1)} copy-done((bf16[1,768,1024]{2,1,0:T(8,128)(2,1)S(1)}, bf16[1,768,1024]{2,1,0:T(8,128)(2,1)}, u32[]{:S(2)}) %copy-start.1) | copy-done | bytes 1572888
  1.5 0.0 copy-start.2
  1.5 1.1 %copy-done.2 = bf16[1,768,512]{2,1,0:T(8,128)(2,1)S(1)} copy-done((bf16[1,768,512]{2,1,0:T(8,128)(2,1)S(1)}, bf16[1,768,512]{2,1,0:T(8,128)(2,1)}, u32[]{:S(2)}) %copy-start.2) | copy-done | bytes 786456
  2.7 0.0 copy-start.3
  2.7 1.1 %copy-done.3 = bf16[384,768]{1,0:T(8,128)(2,1)S(1)} copy-done((bf16[384,768]{1,0:T(8,128)(2,1)S(1)}, bf16[384,768]{1,0:T(8,128)(2,1)}, u32[]{:S(2)}) %copy-start.3) | copy-done | bytes 589848
  3.7 0.0 copy-start.4
  3.7 0.9 copy-done.4
  4.6 0.0 copy-start.5
  4.6 0.9 copy-done.5
  5.5 0.0 copy-start.6
  5.5 0.8 copy-done.6
  6.3 0.0 copy-start.7
  6.3 0.8 copy-done.7
  7.1 0.0 copy-start.8
  7.1 0.8 copy-done.8
  7.8 0.0 copy-start.9
  7.8 0.7 copy-done.9
  8.5 0.0 copy-start.10
  8.5 0.7 copy-done.10
  9.2 0.0 copy-start.11
  9.2 0.7 copy-done.11
  9.9 68.5 %shard_map.127 = (bf16[32,1536]{1,0:T(8,128)(2,1)S(1)}, bf16[16,32,1664]{2,1,0:T(8,128)(2,1)S(1)}, bf16[1,1536,1024]{2,1,0:T(8,128)(2,1)S(1)}, bf16[1,1536,512]{2,1,0:T(8,128)(2,1)S(1)}) custom-call(s32[4]{0:T(128)S(1)} %copy-done.11, bf16[128,384]{1,0:T(8,128)(2,1)S(1)} %copy-done.4, bf16[128,128]{1,0:T(8,128)(2,1)S(1)} %copy-done.7, ...), custom_call_target="tpu_custom_call" | custom-call | tf_op jit(solution)/shard_map/pallas_call | solution.py:393
  78.5 0.2 fusion.9
  78.7 0.2 slice.34
  78.9 1.9 %fusion = f32[512,1024]{1,0:T(8,128)S(1)} fusion(bf16[512,1536]{1,0:T(8,128)(2,1)S(1)} %bitcast.35, bf16[1,1536,1024]{2,1,0:T(8,128)(2,1)S(1)} %get-tuple-element.10), kind=kOutput, calls=%fused_computation | convolution fusion | flops 1610612736 | bytes 6815744 | tf_op jit(solution)/shard_map/dot_general | solution.py:430
  80.8 1.0 multiply_convert_fusion
  81.8 0.0 copy-start.12
  81.8 0.0 copy-done
  81.8 0.4 fusion.3
  82.2 0.7 copy-done.12
  82.9 0.3 convolution_convert_fusion.1
  83.2 19.8 %shard_map.128 = bf16[32,1536]{1,0:T(8,128)(2,1)S(1)} custom-call(bf16[16,32,1536]{2,1,0:T(8,128)(2,1)S(1)} %bitcast.31, bf16[4,32,1536]{2,1,0:T(8,128)(2,1)S(1)} %bitcast.32, bf16[32,1536]{1,0:T(8,128)(2,1)S(1)} %get-tuple-element.12.stream), custom_call_target="tpu_custom_call" | custom-call | tf_op jit(solution)/shard_map/pallas_call | solution.py:444
  103.1 0.6 copy.18
  (4 shorter events, 0.1 us)
Async XLA Ops:
  0.0 81.8 %copy-start = (bf16[1536,2,256]{2,1,0:T(2,128)(2,1)S(1)}, bf16[1536,2,256]{2,1,0:T(2,128)(2,1)}, u32[]{:S(2)}) copy-start(bf16[1536,2,256]{2,1,0:T(2,128)(2,1)} %param.24) | copy-start | bytes 4718596
  0.0 1.5 %copy-start.1 = (bf16[1,768,1024]{2,1,0:T(8,128)(2,1)S(1)}, bf16[1,768,1024]{2,1,0:T(8,128)(2,1)}, u32[]{:S(2)}) copy-start(bf16[1,768,1024]{2,1,0:T(8,128)(2,1)} %gate_up.1) | copy-start | bytes 4718596
  1.5 1.1 %copy-start.2 = (bf16[1,768,512]{2,1,0:T(8,128)(2,1)S(1)}, bf16[1,768,512]{2,1,0:T(8,128)(2,1)}, u32[]{:S(2)}) copy-start(bf16[1,768,512]{2,1,0:T(8,128)(2,1)} %down.1) | copy-start | bytes 2359300
  2.7 1.1 %copy-start.3 = (bf16[384,768]{1,0:T(8,128)(2,1)S(1)}, bf16[384,768]{1,0:T(8,128)(2,1)}, u32[]{:S(2)}) copy-start(bf16[384,768]{1,0:T(8,128)(2,1)} %w_own.1) | copy-start | bytes 1769476
  3.7 0.9 copy-start.4
  4.6 0.9 copy-start.5
  5.5 0.8 copy-start.6
  6.3 0.8 copy-start.7
  7.1 0.8 copy-start.8
  7.8 0.7 copy-start.9
  8.5 0.7 copy-start.10
  9.2 0.7 copy-start.11
  81.8 1.1 %copy-start.12 = (bf16[256,1536]{1,0:T(8,128)(2,1)S(1)}, bf16[256,1536]{1,0:T(8,128)(2,1)}, u32[]{:S(2)}) copy-start(bf16[256,1536]{1,0:T(8,128)(2,1)} %param.25) | copy-start | bytes 2359300

commit v4 on v3

--- a/solution.py
+++ b/solution.py
@@ -217,12 +217,12 @@
 
     att_copy = remote(att, att_other, cross_send, cross_recv, 0, x_peer)
     att_copy.start()
+    bulk_send(2)
     table[...] = jnp.zeros_like(table)
     experts = router.shape[0]
     table[:experts] = router[...]
     table[LOW : LOW + experts] = router[...]
     att_copy.wait()
-    bulk_send(1)
 
     wide = w_own.shape[1]
     own_cols = pl.ds(pl.multiple_of(grp * wide, wide), wide)
@@ -249,11 +249,11 @@
     crossing[...] = total[tok:].astype(jnp.bfloat16)
     cross_copy = remote(crossing, crossed, cross_send, cross_recv, 1, x_peer)
     cross_copy.start()
+    bulk_send(7)
     stream[:, own_cols] = (
         residual[:, own_cols].astype(jnp.float32) + total[:tok]
     ).astype(jnp.bfloat16)
     cross_copy.wait()
-    bulk_send(8)
     stream[:, other_cols] = (
         residual[:, other_cols].astype(jnp.float32) + crossed[...].astype(jnp.float32)
     ).astype(jnp.bfloat16)
@@ -413,7 +413,7 @@
             dma((12,)), dma((12,)), dma((2,)), dma((2,)), dma((2,)),
         ],
         compiler_params=pltpu.CompilerParams(
-            collective_id=0, has_side_effects=True, vmem_limit_bytes=24 * 2**20
+            collective_id=0, has_side_effects=True, vmem_limit_bytes=60 * 2**20
         ),
     )(
         doc_lengths, queries, keys, values, residual_in, w_out, norm_gain,

time: 104 us -> 107 us (1.029)
  Pallas kernels: 88.4 us -> 97.8 us
  local copies, waits for them, and re-layouts: 11.4 us -> 5.32 us
    pallas_call x1, Pallas kernels: 68.5 us -> 81.1 us  [with_kernels(): pl.pallas_call(front_kernel, out_shape=(jax.ShapeDtypeStruct((tok, width)...]
    unnamed x27 -> x13, local copies, waits for them, and re-layouts: 11.2 us -> 3.1 us
    pallas_call x1, Pallas kernels: 19.8 us -> 16.7 us  [with_kernels(): pl.pallas_call(back_kernel, out_shape=jax.ShapeDtypeStruct((tok, width),...]
where the time goes in v4:
time: 107 us
  Pallas kernels  97.8 us (91%)
  local copies, waits for them, and re-layouts  5.32 us (5%)
  matrix products  3.54 us (3%)
    pallas_call x1, Pallas kernels, with_kernels(): pl.pallas_call(front_kernel, out_shape=(jax.ShapeDtypeStruct((tok, width)...  81.1 us
    pallas_call x1, Pallas kernels, with_kernels(): pl.pallas_call(back_kernel, out_shape=jax.ShapeDtypeStruct((tok, width),...  16.7 us
    unnamed x13, local copies, waits for them, and re-layouts  3.1 us

profile of v4, /device:TPU:0, one launch (start us, length us, event | category | flops | bytes accessed | tf_op | source)
XLA Modules:
  0.0 107.1 jit_solution(14665265511993424136)
XLA Ops:
  0.0 0.0 copy-start
  0.0 81.1 %shard_map.127 = (bf16[32,1536]{1,0:T(8,128)(2,1)}, bf16[16,32,1664]{2,1,0:T(8,128)(2,1)}, bf16[1,1536,1024]{2,1,0:T(8,128)(2,1)}, bf16[1,1536,512]{2,1,0:T(8,128)(2,1)}) custom-call(s32[4]{0:T(128)} %lengths.1, bf16[128,384]{1,0:T(8,128)(2,1)} %q.1, bf16[128,128]{1,0:T(8,128)(2,1)} %k.1, bf16[128,128]{1,0:T(8,128)(2,1)} %v.1, bf16[32,1536]{1,0:T(8,128)(2,1)} %residual.1, ...), custom_call_target="tpu_custom_call" | custom-call | tf_op jit(solution)/shard_map/pallas_call | solution.py:393
  81.1 0.0 copy-start.2
  81.1 1.0 slice.31
  82.2 0.2 fusion.9
  82.4 1.0 slice.37
  83.5 0.0 copy-done.2
  83.5 0.0 copy-start.3
  83.5 0.2 slice.34
  83.7 1.7 %copy-done.3 = bf16[1,1536,1024]{2,1,0:T(8,128)(2,1)S(1)} copy-done((bf16[1,1536,1024]{2,1,0:T(8,128)(2,1)S(1)}, bf16[1,1536,1024]{2,1,0:T(8,128)(2,1)}, u32[]{:S(2)}) %copy-start.3) | copy-done | bytes 3145752
  85.4 0.0 copy-start.4
  85.4 1.8 %fusion = f32[512,1024]{1,0:T(8,128)S(1)} fusion(bf16[512,1536]{1,0:T(8,128)(2,1)S(1)} %bitcast.33, bf16[1,1536,1024]{2,1,0:T(8,128)(2,1)S(1)} %copy-done.3), kind=kOutput, calls=%fused_computation | convolution fusion | flops 1610612736 | bytes 6815744 | tf_op jit(solution)/shard_map/dot_general | solution.py:430
  87.2 0.0 copy-done.4
  87.2 1.0 multiply_convert_fusion
  88.3 0.0 copy-start.5
  88.3 0.0 copy-done
  88.3 0.0 copy-start.1
  88.3 0.4 fusion.3
  88.7 0.7 copy-done.5
  89.4 0.3 convolution_convert_fusion.1
  89.7 0.0 copy-done.1
  89.7 16.7 %shard_map.128 = bf16[32,1536]{1,0:T(8,128)(2,1)S(1)} custom-call(bf16[16,32,1536]{2,1,0:T(8,128)(2,1)S(1)} %bitcast.31, bf16[4,32,1536]{2,1,0:T(8,128)(2,1)S(1)} %bitcast.32, bf16[32,1536]{1,0:T(8,128)(2,1)S(1)} %copy-done.1), custom_call_target="tpu_custom_call" | custom-call | tf_op jit(solution)/shard_map/pallas_call | solution.py:444
  106.4 0.6 copy.18
  (2 shorter events, 0.0 us)
Async XLA Ops:
  0.0 88.3 %copy-start = (bf16[1536,2,256]{2,1,0:T(2,128)(2,1)S(1)}, bf16[1536,2,256]{2,1,0:T(2,128)(2,1)}, u32[]{:S(2)}) copy-start(bf16[1536,2,256]{2,1,0:T(2,128)(2,1)} %param.24) | copy-start | bytes 4718596
  81.1 2.3 %copy-start.2 = (bf16[16,32,1664]{2,1,0:T(8,128)(2,1)S(1)}, bf16[16,32,1664]{2,1,0:T(8,128)(2,1)}, u32[]{:S(2)}) copy-start(bf16[16,32,1664]{2,1,0:T(8,128)(2,1)} %get-tuple-element.9) | copy-start | bytes 5111812
  83.5 1.9 %copy-start.3 = (bf16[1,1536,1024]{2,1,0:T(8,128)(2,1)S(1)}, bf16[1,1536,1024]{2,1,0:T(8,128)(2,1)}, u32[]{:S(2)}) copy-start(bf16[1,1536,1024]{2,1,0:T(8,128)(2,1)} %get-tuple-element.10) | copy-start | bytes 9437188
  85.4 1.9 %copy-start.4 = (bf16[1,1536,512]{2,1,0:T(8,128)(2,1)S(1)}, bf16[1,1536,512]{2,1,0:T(8,128)(2,1)}, u32[]{:S(2)}) copy-start(bf16[1,1536,512]{2,1,0:T(8,128)(2,1)} %get-tuple-element.11) | copy-start | bytes 4718596
  88.3 1.1 %copy-start.5 = (bf16[256,1536]{1,0:T(8,128)(2,1)S(1)}, bf16[256,1536]{1,0:T(8,128)(2,1)}, u32[]{:S(2)}) copy-start(bf16[256,1536]{1,0:T(8,128)(2,1)} %param.25) | copy-start | bytes 2359300
  88.3 1.4 %copy-start.1 = (bf16[32,1536]{1,0:T(8,128)(2,1)S(1)}, bf16[32,1536]{1,0:T(8,128)(2,1)}, u32[]{:S(2)}) copy-start(bf16[32,1536]{1,0:T(8,128)(2,1)} %get-tuple-element.12.stream) | copy-start | bytes 294916

commit v5 on v4

--- a/solution.py
+++ b/solution.py
@@ -129,8 +129,8 @@
 
 def front_kernel(
     lengths, q, k, v, residual, w_own, gain, router, ids, gate_up, down,
-    stream, gathered, gate_full, down_full,
-    kv, att, att_other, partial, arrived, crossing, crossed, table,
+    stream, tokens, coded, gate_full, down_full,
+    gathered, kv, att, att_other, partial, arrived, crossing, crossed, table,
     kv_send, kv_recv, sum_send, sum_recv, tok_send, tok_recv, big_send, big_recv, cross_send, cross_recv,
     local_sem,
 ):
@@ -180,7 +180,7 @@
             copy.start()
             bulk.append(copy)
 
-    bulk_send(3)
+    bulk_send(2)
     mine = pl.ds(pl.multiple_of(grp * half, half), half)
     gate_local = pltpu.make_async_copy(gate_up, gate_full.at[:, mine], local_sem.at[0])
     down_local = pltpu.make_async_copy(down, down_full.at[:, mine], local_sem.at[1])
@@ -217,7 +217,7 @@
 
     att_copy = remote(att, att_other, cross_send, cross_recv, 0, x_peer)
     att_copy.start()
-    bulk_send(2)
+    bulk_send(1)
     table[...] = jnp.zeros_like(table)
     experts = router.shape[0]
     table[:experts] = router[...]
@@ -241,6 +241,7 @@
             )
             copy.start()
             sums.append(copy)
+    bulk_send(1)
     total = partial[0].astype(jnp.float32)
     for copy in sums:
         copy.wait()
@@ -249,7 +250,7 @@
     crossing[...] = total[tok:].astype(jnp.bfloat16)
     cross_copy = remote(crossing, crossed, cross_send, cross_recv, 1, x_peer)
     cross_copy.start()
-    bulk_send(7)
+    bulk_send(1)
     stream[:, own_cols] = (
         residual[:, own_cols].astype(jnp.float32) + total[:tok]
     ).astype(jnp.bfloat16)
@@ -296,17 +297,23 @@
         return copy
 
     first = {by: passing(0, by, at_exp(by)) for by in (2, 1, 3)}
+    bulk_send(1)
     second, third = {}, []
     for by in (0, 1, 2, 3):
         if by:
             first[by].wait_recv()
         second[by] = passing(by, 8 + by, y_peer)
         third.append(passing(by, 4 + by, core_peer))
+        if by:
+            bulk_send(1)
     for by in (0, 1, 2, 3):
         second[by].wait_recv()
         third.append(passing(8 + by, 12 + by, core_peer))
+    bulk_send(3)
     for copy in third:
         copy.wait_recv()
+    tokens[...] = gathered[:, :, :width]
+    coded[...] = gathered[:, :, width:]
     for copy in [*first.values(), *second.values(), *third]:
         copy.wait_send()
     gate_local.wait()
@@ -390,17 +397,19 @@
     smem = pl.BlockSpec(memory_space=pltpu.SMEM)
     dma = pltpu.SemaphoreType.DMA
     up_shape, down_shape = expert_gate_up.shape, expert_down.shape
-    stream, gathered, gate_full, down_full = pl.pallas_call(
+    stream, tokens, coded, gate_full, down_full = pl.pallas_call(
         front_kernel,
         out_shape=(
             jax.ShapeDtypeStruct((tok, width), bf),
-            jax.ShapeDtypeStruct((16, tok, width + LANES), bf),
+            jax.ShapeDtypeStruct((16, tok, width), bf),
+            jax.ShapeDtypeStruct((16, tok, LANES), bf),
             jax.ShapeDtypeStruct((up_shape[0], 2 * up_shape[1], up_shape[2]), bf),
             jax.ShapeDtypeStruct((down_shape[0], 2 * down_shape[1], down_shape[2]), bf),
         ),
         in_specs=[smem, *[vmem] * 8, hbm, hbm],
-        out_specs=(vmem, vmem, hbm, hbm),
+        out_specs=(vmem, vmem, vmem, hbm, hbm),
         scratch_shapes=[
+            pltpu.VMEM((16, tok, width + LANES), bf),
             pltpu.VMEM((3, 2, rows, HEAD), bf),
             pltpu.VMEM((rows, heads_dev), bf),
             pltpu.VMEM((rows, heads_dev), bf),
@@ -419,8 +428,8 @@
         doc_lengths, queries, keys, values, residual_in, w_out, norm_gain,
         router.T, expert_ids.T, expert_gate_up, expert_down,
     )
-    tokens = gathered[:, :, :width].reshape(16 * tok, width)
-    coded = gathered[:, :, width:].reshape(16 * tok, LANES).astype(jnp.float32)
+    tokens = tokens.reshape(16 * tok, width)
+    coded = coded.reshape(16 * tok, LANES).astype(jnp.float32)
     gates = coded[:, :LOW] + coded[:, LOW:]
     local = up_shape[0]
     first = (lax.axis_index("ctx") * lax.axis_size("exp") + lax.axis_index("exp")) * local

time: 107 us -> 107 us (level)
  local copies, waits for them, and re-layouts: 5.32 us -> 1.98 us
  matrix products: 3.54 us -> 6 us
    dot_general x1, matrix products: 1.85 us -> 4.27 us  [with_kernels(): pre = jnp.dot(tokens, gate_full[e], preferred_element_type=jnp.float32)]
    unnamed x13 -> x9, local copies, waits for them, and re-layouts: 3.1 us -> 0.89 us
    slice x2 -> x0, local copies, waits for them, and re-layouts: 1.2 us -> none  [the longest x1 1.04 us: with_kernels(): coded = gathered[:, :, width:].reshape(16 * tok, LANES).astype(jnp.float32)]
where the time goes in v5:
time: 107 us
  Pallas kernels  97.7 us (91%)
  matrix products  6 us (6%)
  local copies, waits for them, and re-layouts  1.98 us (2%)
  other arithmetic  1.16 us (1%)
    pallas_call x1, Pallas kernels, with_kernels(): pl.pallas_call(front_kernel, out_shape=(jax.ShapeDtypeStruct((tok, width)...  81.1 us
    pallas_call x1, Pallas kernels, with_kernels(): pl.pallas_call(back_kernel, out_shape=jax.ShapeDtypeStruct((tok, width),...  16.6 us
    dot_general x1, matrix products, with_kernels(): pre = jnp.dot(tokens, gate_full[e], preferred_element_type=jnp.float32)  4.27 us

profile of v5, /device:TPU:0, one launch (start us, length us, event | category | flops | bytes accessed | tf_op | source)
XLA Modules:
  0.0 107.0 jit_solution(14710818623783736886)
XLA Ops:
  0.0 0.0 copy-start
  0.0 81.1 %shard_map.127 = (bf16[32,1536]{1,0:T(8,128)(2,1)}, bf16[16,32,1536]{2,1,0:T(8,128)(2,1)}, bf16[16,32,128]{2,1,0:T(8,128)(2,1)}, bf16[1,1536,1024]{2,1,0:T(8,128)(2,1)}, bf16[1,1536,512]{2,1,0:T(8,128)(2,1)}) custom-call(s32[4]{0:T(128)} %lengths.1, bf16[128,384]{1,0:T(8,128)(2,1)} %q.1, bf16[128,128]{1,0:T(8,128)(2,1)} %k.1, bf16[128,128]{1,0:T(8,128)(2,1)} %v.1, ...), custom_call_target="tpu_custom_call" | custom-call | tf_op jit(solution)/shard_map/pallas_call | solution.py:400
  81.1 0.9 convert.1
  82.1 0.2 fusion.9
  82.3 0.0 copy-start.2
  82.3 4.3 %fusion = f32[512,1024]{1,0:T(8,128)S(1)} fusion(bf16[512,1536]{1,0:T(8,128)(2,1)} %bitcast.35, bf16[1,1536,1024]{2,1,0:T(8,128)(2,1)} %get-tuple-element.12), kind=kOutput, calls=%fused_computation | convolution fusion | flops 1610612736 | bytes 6815744 | tf_op jit(solution)/shard_map/dot_general | solution.py:439
  86.6 0.0 copy-done.2
  86.6 1.1 multiply_convert_fusion
  87.7 0.0 copy-start.3
  87.7 1.1 %slice.28 = bf16[4,32,1536]{2,1,0:T(8,128)(2,1)S(1)} slice(bf16[16,32,1536]{2,1,0:T(8,128)(2,1)} %get-tuple-element.11), slice={[0:4], [0:32], [0:1536]} | slice | bytes 786432 | tf_op jit(solution)/shard_map/slice | solution.py:447
  88.8 0.0 copy-done
  88.8 0.0 copy-start.1
  88.8 0.4 fusion.3
  89.2 0.0 copy-done.3
  89.2 0.3 convolution_convert_fusion.1
  89.5 0.2 copy-done.1
  89.7 16.6 %shard_map.128 = bf16[32,1536]{1,0:T(8,128)(2,1)S(1)} custom-call(bf16[16,32,1536]{2,1,0:T(8,128)(2,1)S(1)} %bitcast.31, bf16[4,32,1536]{2,1,0:T(8,128)(2,1)S(1)} %bitcast.32, bf16[32,1536]{1,0:T(8,128)(2,1)S(1)} %copy-done.1), custom_call_target="tpu_custom_call" | custom-call | tf_op jit(solution)/shard_map/pallas_call | solution.py:453
  106.4 0.6 copy.18
  (1 shorter events, 0.0 us)
Async XLA Ops:
  0.0 88.8 %copy-start = (bf16[1536,2,256]{2,1,0:T(2,128)(2,1)S(1)}, bf16[1536,2,256]{2,1,0:T(2,128)(2,1)}, u32[]{:S(2)}) copy-start(bf16[1536,2,256]{2,1,0:T(2,128)(2,1)} %param.24) | copy-start | bytes 4718596
  82.3 4.3 %copy-start.2 = (bf16[1,1536,512]{2,1,0:T(8,128)(2,1)S(1)}, bf16[1,1536,512]{2,1,0:T(8,128)(2,1)}, u32[]{:S(2)}) copy-start(bf16[1,1536,512]{2,1,0:T(8,128)(2,1)} %get-tuple-element.13) | copy-start | bytes 4718596
  87.7 1.5 %copy-start.3 = (bf16[256,1536]{1,0:T(8,128)(2,1)S(1)}, bf16[256,1536]{1,0:T(8,128)(2,1)}, u32[]{:S(2)}) copy-start(bf16[256,1536]{1,0:T(8,128)(2,1)} %param.25) | copy-start | bytes 2359300
  88.8 0.9 copy-start.1

commit v6 on v5

--- a/solution.py
+++ b/solution.py
@@ -422,7 +422,7 @@
             dma((12,)), dma((12,)), dma((2,)), dma((2,)), dma((2,)),
         ],
         compiler_params=pltpu.CompilerParams(
-            collective_id=0, has_side_effects=True, vmem_limit_bytes=60 * 2**20
+            collective_id=0, has_side_effects=True, vmem_limit_bytes=24 * 2**20
         ),
     )(
         doc_lengths, queries, keys, values, residual_in, w_out, norm_gain,

time: 107 us -> 103 us (0.963)
  Pallas kernels: 97.7 us -> 82.8 us
  local copies, waits for them, and re-layouts: 1.98 us -> 14 us
    pallas_call x1, Pallas kernels: 81.1 us -> 62.8 us  [with_kernels(): pl.pallas_call(front_kernel, out_shape=(jax.ShapeDtypeStruct((tok, width)...]
    unnamed x9 -> x33, local copies, waits for them, and re-layouts: 0.89 us -> 14 us
    pallas_call x1, Pallas kernels: 16.6 us -> 20 us  [with_kernels(): pl.pallas_call(back_kernel, out_shape=jax.ShapeDtypeStruct((tok, width),...]
where the time goes in v6:
time: 103 us
  Pallas kernels  82.8 us (80%)
  local copies, waits for them, and re-layouts  14 us (14%)
  matrix products  5.49 us (5%)
    pallas_call x1, Pallas kernels, with_kernels(): pl.pallas_call(front_kernel, out_shape=(jax.ShapeDtypeStruct((tok, width)...  62.8 us
    pallas_call x1, Pallas kernels, with_kernels(): pl.pallas_call(back_kernel, out_shape=jax.ShapeDtypeStruct((tok, width),...  20 us
    unnamed x33, local copies, waits for them, and re-layouts  14 us
    dot_general x1, matrix products, with_kernels(): pre = jnp.dot(tokens, gate_full[e], preferred_element_type=jnp.float32)  3.8 us

profile of v6, /device:TPU:0, one launch (start us, length us, event | category | flops | bytes accessed | tf_op | source)
XLA Modules:
  0.0 102.6 jit_solution(3174053301392917584)
XLA Ops:
  0.0 0.0 copy-start
  0.0 0.0 copy-start.1
  0.0 1.5 %copy-done.1 = bf16[1,768,1024]{2,1,0:T(8,128)(2,1)S(1)} copy-done((bf16[1,768,1024]{2,1,0:T(8,128)(2,1)S(1)}, bf16[1,768,1024]{2,1,0:T(8,128)(2,1)}, u32[]{:S(2)}) %copy-start.1) | copy-done | bytes 1572888
  1.5 0.0 copy-start.2
  1.5 1.1 %copy-done.2 = bf16[1,768,512]{2,1,0:T(8,128)(2,1)S(1)} copy-done((bf16[1,768,512]{2,1,0:T(8,128)(2,1)S(1)}, bf16[1,768,512]{2,1,0:T(8,128)(2,1)}, u32[]{:S(2)}) %copy-start.2) | copy-done | bytes 786456
  2.7 0.0 copy-start.3
  2.7 1.1 %copy-done.3 = bf16[384,768]{1,0:T(8,128)(2,1)S(1)} copy-done((bf16[384,768]{1,0:T(8,128)(2,1)S(1)}, bf16[384,768]{1,0:T(8,128)(2,1)}, u32[]{:S(2)}) %copy-start.3) | copy-done | bytes 589848
  3.7 0.0 copy-start.4
  3.7 0.9 copy-done.4
  4.6 0.0 copy-start.5
  4.6 0.9 copy-done.5
  5.5 0.0 copy-start.6
  5.5 0.8 copy-done.6
  6.3 0.0 copy-start.7
  6.3 0.8 copy-done.7
  7.1 0.0 copy-start.8
  7.1 0.8 copy-done.8
  7.8 0.0 copy-start.9
  7.8 0.7 copy-done.9
  8.5 0.0 copy-start.10
  8.5 0.7 copy-done.10
  9.2 0.0 copy-start.11
  9.2 0.7 copy-done.11
  9.9 62.8 %shard_map.127 = (bf16[32,1536]{1,0:T(8,128)(2,1)S(1)}, bf16[16,32,1536]{2,1,0:T(8,128)(2,1)S(1)}, bf16[16,32,128]{2,1,0:T(8,128)(2,1)S(1)}, bf16[1,1536,1024]{2,1,0:T(8,128)(2,1)S(1)}, bf16[1,1536,512]{2,1,0:T(8,128)(2,1)S(1)}) custom-call(s32[4]{0:T(128)S(1)} %copy-done.11, bf16[128,384]{1,0:T(8,128)(2,1)S(1)} %copy-done.4, ...), custom_call_target="tpu_custom_call" | custom-call | tf_op jit(solution)/shard_map/pallas_call | solution.py:400
  72.7 0.0 copy-start.12
  72.7 1.6 %copy-done.12 = bf16[1,1536,1024]{2,1,0:T(8,128)(2,1)} copy-done((bf16[1,1536,1024]{2,1,0:T(8,128)(2,1)}, bf16[1,1536,1024]{2,1,0:T(8,128)(2,1)S(1)}, u32[]{:S(2)}) %copy-start.12) | copy-done | bytes 3145752
  74.3 0.0 copy-start.13
  74.3 1.1 %copy-done.13 = bf16[1,1536,512]{2,1,0:T(8,128)(2,1)} copy-done((bf16[1,1536,512]{2,1,0:T(8,128)(2,1)}, bf16[1,1536,512]{2,1,0:T(8,128)(2,1)S(1)}, u32[]{:S(2)}) %copy-start.13) | copy-done | bytes 1572888
  75.5 0.2 fusion.9
  75.7 0.0 copy-start.14
  75.7 3.8 %fusion = f32[512,1024]{1,0:T(8,128)S(1)} fusion(bf16[512,1536]{1,0:T(8,128)(2,1)S(1)} %bitcast.34, bf16[1,1536,1024]{2,1,0:T(8,128)(2,1)} %copy-done.12), kind=kOutput, calls=%fused_computation | convolution fusion | flops 1610612736 | bytes 6815744 | tf_op jit(solution)/shard_map/dot_general | solution.py:439
  79.5 0.0 copy-done.14
  79.5 1.0 %multiply_convert_fusion = bf16[512,1536]{1,0:T(8,128)(2,1)S(1)} fusion(bf16[1,1536,512]{2,1,0:T(8,128)(2,1)S(1)} %copy-done.14, f32[512]{0:T(512)S(1)} %fusion.9, f32[512,1024]{1,0:T(8,128)S(1)} %fusion), kind=kOutput, calls=%fused_computation.2 | convolution fusion | flops 810024960 | bytes 5244928 | tf_op jit(solution)/shard_map/dot_general | solution.py:441
  80.6 0.0 copy-start.15
  80.6 0.0 copy-done
  80.6 0.4 fusion.3
  81.0 0.7 copy-done.15
  81.7 0.3 convolution_convert_fusion.1
  82.0 20.0 %shard_map.128 = bf16[32,1536]{1,0:T(8,128)(2,1)S(1)} custom-call(bf16[16,32,1536]{2,1,0:T(8,128)(2,1)S(1)} %bitcast.31, bf16[4,32,1536]{2,1,0:T(8,128)(2,1)S(1)} %bitcast.32, bf16[32,1536]{1,0:T(8,128)(2,1)S(1)} %get-tuple-element.14.stream), custom_call_target="tpu_custom_call" | custom-call | tf_op jit(solution)/shard_map/pallas_call | solution.py:453
  102.0 0.6 copy.18
  (3 shorter events, 0.1 us)
Async XLA Ops:
  0.0 80.6 %copy-start = (bf16[1536,2,256]{2,1,0:T(2,128)(2,1)S(1)}, bf16[1536,2,256]{2,1,0:T(2,128)(2,1)}, u32[]{:S(2)}) copy-start(bf16[1536,2,256]{2,1,0:T(2,128)(2,1)} %param.24) | copy-start | bytes 4718596
  0.0 1.5 %copy-start.1 = (bf16[1,768,1024]{2,1,0:T(8,128)(2,1)S(1)}, bf16[1,768,1024]{2,1,0:T(8,128)(2,1)}, u32[]{:S(2)}) copy-start(bf16[1,768,1024]{2,1,0:T(8,128)(2,1)} %gate_up.1) | copy-start | bytes 4718596
  1.5 1.1 %copy-start.2 = (bf16[1,768,512]{2,1,0:T(8,128)(2,1)S(1)}, bf16[1,768,512]{2,1,0:T(8,128)(2,1)}, u32[]{:S(2)}) copy-start(bf16[1,768,512]{2,1,0:T(8,128)(2,1)} %down.1) | copy-start | bytes 2359300
  2.7 1.1 %copy-start.3 = (bf16[384,768]{1,0:T(8,128)(2,1)S(1)}, bf16[384,768]{1,0:T(8,128)(2,1)}, u32[]{:S(2)}) copy-start(bf16[384,768]{1,0:T(8,128)(2,1)} %w_own.1) | copy-start | bytes 1769476
  3.7 0.9 copy-start.4
  4.6 0.9 copy-start.5
  5.5 0.8 copy-start.6
  6.3 0.8 copy-start.7
  7.1 0.8 copy-start.8
  7.8 0.7 copy-start.9
  8.5 0.7 copy-start.10
  9.2 0.7 copy-start.11
  72.7 1.6 %copy-start.12 = (bf16[1,1536,1024]{2,1,0:T(8,128)(2,1)}, bf16[1,1536,1024]{2,1,0:T(8,128)(2,1)S(1)}, u32[]{:S(2)}) copy-start(bf16[1,1536,1024]{2,1,0:T(8,128)(2,1)S(1)} %get-tuple-element.12) | copy-start | bytes 9437188
  74.3 1.2 %copy-start.13 = (bf16[1,1536,512]{2,1,0:T(8,128)(2,1)}, bf16[1,1536,512]{2,1,0:T(8,128)(2,1)S(1)}, u32[]{:S(2)}) copy-start(bf16[1,1536,512]{2,1,0:T(8,128)(2,1)S(1)} %get-tuple-element.13) | copy-start | bytes 4718596
  75.7 3.8 %copy-start.14 = (bf16[1,1536,512]{2,1,0:T(8,128)(2,1)S(1)}, bf16[1,1536,512]{2,1,0:T(8,128)(2,1)}, u32[]{:S(2)}) copy-start(bf16[1,1536,512]{2,1,0:T(8,128)(2,1)} %copy-done.13) | copy-start | bytes 4718596
  80.6 1.1 %copy-start.15 = (bf16[256,1536]{1,0:T(8,128)(2,1)S(1)}, bf16[256,1536]{1,0:T(8,128)(2,1)}, u32[]{:S(2)}) copy-start(bf16[256,1536]{1,0:T(8,128)(2,1)} %param.25) | copy-start | bytes 2359300
